TPU v7x, 32 devices: a whole 2x2x4 slice. The times are simulated.
32 devices in a mesh: wide: 8 (over z, x), narrow: 4 (over y, core).
Axes of the slice: x: 2, y: 2, z: 4, core: 2. Of those that a mesh axis runs over, the one named last changes fastest.
Arguments:
- amplitudes: float32 [16384, 1024], P('wide', 'narrow'), may hold values from -6 to 6
- ladder_blocks: float32 [128, 16, 128, 128], P('wide'), may hold values from -0.125 to 0.125
- ladder_index: int32 [128, 16], P('wide'), may hold values from 0 to 127, all different within a row
- cycle_blocks: float32 [32, 16, 128, 128], P(None, 'narrow'), may hold values from -0.125 to 0.125
- cycle_index: int32 [32, 16], P(None, 'narrow'), may hold values from 0 to 31, all different within a row
- eps_virt: float32 [128], replicated, may hold values from 0.3 to 1.5
- eps_occ: float32 [32], replicated, may hold values from -0.7 to -0.2
Outputs:
- new_amplitudes: float32 [16384, 1024], P('wide', 'narrow')
Inputs may be any that keep to these rules, and one draw needn't show every extreme that they name: `ladder_index`: each row lists 16 different virtual indices, and every virtual index is listed by some row. `cycle_index`: each row lists 16 different occupied indices, and every occupied index is listed by some row.
All inputs are finite; a program needn't handle non-finite values.
Results may differ from a plain program's by a relative error of at most 0.000052.
Values sent between devices are 32-bit elements; how exact they have to be, the bound alone decides.
No kernel may reach another device: no remote copies, remote signals or barrier semaphores. Data moves between devices by JAX's collectives and lax.ppermute only.
A program may use at most 192 MiB of HBM per device.

v0:
```python
import jax
import jax.numpy as jnp
from jax import lax
from jax.sharding import PartitionSpec as P


def per_device(
    amplitudes, ladder_blocks, ladder_index, cycle_blocks, cycle_index, eps_virt, eps_occ
):
    virt = eps_virt.shape[0]
    occ = eps_occ.shape[0]
    rows_here = amplitudes.shape[0]
    cols_here = amplitudes.shape[1]
    a_here = rows_here // virt
    i_here = cols_here // occ
    b_here = virt // lax.axis_size("wide")
    wide_pos = lax.axis_index("wide")
    narrow_pos = lax.axis_index("narrow")
    mine = None
    gathered = lax.all_gather(amplitudes, "wide", axis=0, tiled=True)
    taken = jnp.take(gathered.reshape(virt, virt, cols_here), ladder_index, axis=0)
    mine = lax.dynamic_slice_in_dim(
        gathered.reshape(virt, virt, i_here, occ), wide_pos * b_here, b_here, 1
    )
    ladder = jnp.einsum("akbd,akdn->abn", ladder_blocks, taken, precision=lax.Precision.HIGHEST)
    every_k = lax.all_gather(mine, "narrow", axis=2, tiled=True)
    by_occupied = every_k.transpose(2, 0, 1, 3).reshape(occ, virt, b_here * occ)
    picked = jnp.take(by_occupied, cycle_index, axis=0)
    terms = jnp.einsum("isac,iscn->ian", cycle_blocks, picked, precision=lax.Precision.HIGHEST)
    cycle_mine = lax.psum_scatter(
        terms.reshape(i_here * virt * lax.axis_size("narrow"), b_here * occ),
        "narrow",
        scatter_dimension=0,
        tiled=True,
    )
    cycle_four = cycle_mine.reshape(i_here, virt, b_here, occ)
    cycle_pairs = lax.all_to_all(cycle_four, "wide", split_axis=1, concat_axis=2, tiled=True)
    cycle = cycle_pairs.transpose(1, 2, 0, 3).reshape(rows_here, cols_here)
    energy_a = lax.dynamic_slice_in_dim(eps_virt, wide_pos * a_here, a_here, 0)
    energy_i = lax.dynamic_slice_in_dim(eps_occ, narrow_pos * i_here, i_here, 0)
    denominator = (
        energy_a[:, None, None, None]
        + eps_virt[None, :, None, None]
        - energy_i[None, None, :, None]
        - eps_occ[None, None, None, :]
    )
    total = ladder.reshape(rows_here, cols_here) + cycle
    return total / denominator.reshape(rows_here, cols_here)


def solution(mesh):
    in_specs = (
        P("wide", "narrow"),
        P("wide", None, None, None),
        P("wide", None),
        P(None, "narrow", None, None),
        P(None, "narrow"),
        P(),
        P(),
    )
    out_specs = P("wide", "narrow")
    return jax.shard_map(
        per_device, mesh=mesh, in_specs=in_specs, out_specs=out_specs, check_vma=False
    )
```

profile of v0, /device:TPU:0, one launch (start us, length us, event | category | flops | bytes accessed | tf_op | source)
XLA Modules:
  0.0 614.4 jit_solution(2741345188687390025)
XLA Ops:
  6.5 0.0 all-gather.3.cloned.1.call-start
  6.5 0.7 all-gather.3.cloned.1.call-update
  7.3 0.0 all-gather.5.cloned.1.call-start
  7.3 232.5 %all-gather.3.cloned.1.call-done = f32[16384,256]{1,0:T(8,128)} async-done(((f32[2048,256]{1,0:T(8,128)}), f32[16384,256]{1,0:T(8,128)}) %all-gather.3.cloned.1.call-update) | async-done | bytes 16777232 | tf_op jit(solution)/shard_map/all_gather | solution.py:20
  239.8 17.4 %copy.44 = f32[16384,256]{0,1:T(8,128)} copy(f32[16384,256]{1,0:T(8,128)} %all-gather.3.cloned.1.call-done) | data formatting | bytes 33554432 | tf_op jit(solution)/shard_map/all_gather | solution.py:20
  257.2 9.4 %copy.58 = f32[32,8,128,128]{3,2,1,0:T(8,128)S(1)} copy(f32[32,8,128,128]{3,1,2,0:T(8,128)} %bitcast.59) | data formatting | bytes 33554432
  266.6 7.5 %constant_dynamic-slice_fusion = f32[128,16,8,32]{1,0,3,2:T(8,128)} fusion(f32[128,128,8,32]{1,0,3,2:T(8,128)S(1)} %bitcast.58, s32[]{:T(128)S(6)} %select_n.28), kind=kLoop, calls=%fused_computation.21 | loop fusion | bytes 4194308 | tf_op jit(solution)/shard_map/dynamic_slice | solution.py:22
  274.1 0.0 copy-start.1
  274.1 11.0 %copy.45 = f32[128,16,8,32]{0,3,1,2:T(8,128)} copy(f32[128,16,8,32]{1,0,3,2:T(8,128)} %constant_dynamic-slice_fusion) | data formatting | bytes 4194304 | tf_op jit(solution)/shard_map/dynamic_slice | solution.py:22
  285.1 0.0 all-gather.5.cloned.1.call-update
  285.2 0.2 reduce-scatter.2.cloned.1.call-start
  285.4 0.0 copy-done.1
  285.4 0.1 copy.46
  285.5 0.1 reshape.91
  285.6 0.1 copy.43
  285.7 56.1 %all-gather.5.cloned.1.call-done = f32[128,16,32,32]{0,3,1,2:T(8,128)} async-done(((f32[128,16,8,32]{0,3,1,2:T(8,128)}), f32[128,16,32,32]{0,3,1,2:T(8,128)}) %all-gather.5.cloned.1.call-update) | async-done | bytes 8388624 | tf_op jit(solution)/shard_map/all_gather | solution.py:26
  341.8 17.2 %gather_fusion.1 = f32[128,128,512]{1,2,0:T(8,128)} fusion(f32[32,128,512]{1,2,0:T(8,128)} %bitcast.56, s32[1024]{0:T(1024)S(1)} %pad_clamp_fusion), kind=kCustom, calls=%fused_computation.1 | custom fusion | bytes 67109376 | tf_op jit(solution)/shard_map/jit(_take)/gather | solution.py:28
  359.0 33.4 %copy.47 = f32[32,4,128,512]{3,2,1,0:T(8,128)} copy(f32[32,4,128,512]{2,3,1,0:T(8,128)} %bitcast.57) | data formatting | bytes 67108864 | tf_op jit(solution)/shard_map/jit(_take)/gather | solution.py:28
  392.4 25.6 %fusion = f32[32,512,128,1]{1,2,3,0:T(8,128)} fusion(f32[32,4,128,128]{3,2,1,0:T(8,128)} %param.10, f32[32,4,128,512]{3,2,1,0:T(8,128)} %copy.47, pred[32,4]{1,0:T(8,128)(4,1)S(1)} %copy.43), kind=kOutput, calls=%fused_computation.2 | convolution fusion | flops 12893290496 | bytes 50331776 | tf_op jit(solution)/shard_map/isac,iscn->ian/dot_general | solution.py:29
  418.1 8.9 %copy.48 = f32[4096,512]{0,1:T(8,128)} copy(f32[4096,512]{1,0:T(8,128)} %bitcast.60) | data formatting | bytes 16777216 | tf_op jit(solution)/shard_map/reshape | solution.py:31
  427.0 0.0 reduce-scatter.2.cloned.1.call-update
  427.0 71.9 %reduce-scatter.2.cloned.1.call-done = f32[1024,512]{0,1:T(8,128)} async-done(((f32[4096,512]{0,1:T(8,128)}), f32[1024,512]{0,1:T(8,128)}) %reduce-scatter.2.cloned.1.call-update) | async-done | bytes 2097168 | tf_op jit(solution)/shard_map/reduce_scatter | solution.py:30
  498.9 2.1 copy.59
  500.9 8.1 %copy.49 = f32[8,128,16,32]{3,2,0,1:T(8,128)} copy(f32[8,128,16,32]{1,0,3,2:T(8,128)S(1)} %bitcast.67) | data formatting | bytes 4194304 | tf_op jit(solution)/shard_map/reshape | solution.py:36
  509.1 0.0 copy-start.3
  509.1 0.0 copy-start
  509.1 0.0 copy-start.2
  509.1 8.6 %reshape.103 = f32[8,1,65536]{2,1,0:T(1,128)} reshape(f32[128,8,16,32]{3,2,1,0:T(8,128)} %bitcast.61) | data formatting | bytes 4194304
  517.7 5.5 all-to-all-start
  523.2 0.0 copy-done.3
  523.2 0.1 dynamic_slice.10
  523.3 0.0 copy-done
  523.3 0.1 reshape.83
  523.4 0.0 copy-done.2
  523.4 0.1 dynamic_slice.11
  523.5 0.1 sub.44
  523.5 0.1 broadcast_add_fusion
  523.6 0.1 broadcast_subtract_fusion
  523.7 20.7 %gather_fusion = f32[256,128,256]{2,1,0:T(8,128)} fusion(f32[128,128,256]{2,1,0:T(8,128)} %bitcast.55, s32[1024]{0:T(1024)S(1)} %pad_clamp_fusion.1), kind=kCustom, calls=%fused_computation | custom fusion | bytes 67109888 | tf_op jit(solution)/shard_map/jit(_take)/gather | solution.py:21
  544.4 26.6 %fusion.2 = f32[16,256,128,1]{1,2,3,0:T(8,128)S(1)} fusion(f32[16,16,128,128]{3,2,1,0:T(8,128)} %param.8, f32[16,16,128,256]{3,2,1,0:T(8,128)} %bitcast.54, pred[16,16]{1,0:T(8,128)(4,1)S(1)} %compare_and_fusion), kind=kOutput, calls=%fused_computation.4 | convolution fusion | flops 12893290496 | bytes 52429056 | tf_op jit(solution)/shard_map/akbd,akdn->abn/dot_general | solution.py:25
  571.0 1.8 copy.53
  572.8 0.0 all-to-all-done
  572.8 0.6 broadcast.54
  573.4 7.2 %reduce = f32[8,65536]{1,0:T(8,128)S(1)} reduce(f32[8,1,65536]{2,1,0:T(1,128)} %all-to-all-done, f32[]{:T(128)} %broadcast.54), dimensions={1}, to_apply=%all_to_all.13.reduce_sub_computation | reduce | bytes 4194308 | tf_op jit(solution)/shard_map/all_to_all | solution.py:37
  580.6 6.0 reshape.104
  586.6 7.9 %copy.51 = f32[8,16,8,16,32]{4,3,2,1,0:T(8,128)} copy(f32[8,16,8,16,32]{4,3,0,1,2:T(8,128)} %bitcast.62) | data formatting | bytes 4194304 | tf_op jit(solution)/shard_map/all_to_all | solution.py:37
  594.5 5.2 copy.52
  599.7 0.2 sub.41
  599.9 5.1 fusion.8
  605.0 2.9 copy.54
  (7 shorter events, 0.0 us)
Async XLA Ops:
  6.5 233.3 %all-gather.3.cloned.1.call-start = ((), (), s32[]{:S(2)}) async-start(), calls=%async_computation.2 | async-start | bytes 18874368 | tf_op jit(solution)/shard_map/all_gather | solution.py:20
  7.3 334.5 %all-gather.5.cloned.1.call-start = ((), (), s32[]{:S(2)}) async-start(), calls=%async_computation.3 | async-start | bytes 10485760 | tf_op jit(solution)/shard_map/all_gather | solution.py:26
  274.1 11.3 %copy-start.1 = (s32[32,4]{0,1:T(4,128)S(1)}, s32[32,4]{0,1:T(4,128)}, u32[]{:S(2)}) copy-start(s32[32,4]{0,1:T(4,128)} %param.11) | copy-start | bytes 1540
  285.2 213.7 %reduce-scatter.2.cloned.1.call-start = ((), (), s32[]{:S(2)}) async-start(), calls=%async_computation.4 | async-start | bytes 10485760 | tf_op jit(solution)/shard_map/reduce_scatter | solution.py:30
  509.1 14.1 %copy-start.3 = (f32[128]{0:T(128)S(1)}, f32[128]{0:T(128)}, u32[]{:S(2)}) copy-start(f32[128]{0:T(128)} %param.12) | copy-start | bytes 1540
  509.1 14.2 %copy-start = (s32[16,16]{1,0:T(8,128)S(1)}, s32[16,16]{1,0:T(8,128)}, u32[]{:S(2)}) copy-start(s32[16,16]{1,0:T(8,128)} %param.9) | copy-start | bytes 3076
  509.1 14.3 %copy-start.2 = (f32[32]{0:T(128)S(1)}, f32[32]{0:T(128)}, u32[]{:S(2)}) copy-start(f32[32]{0:T(128)} %param.13) | copy-start | bytes 388
  517.7 55.1 %all-to-all-start = ((f32[8,1,65536]{2,1,0:T(1,128)}), f32[8,1,65536]{2,1,0:T(1,128)}, u32[]{:S(2)}, u32[]{:S(2)}) async-start(f32[8,1,65536]{2,1,0:T(1,128)} %reshape.103), calls=%async_computation.1 | async-start | bytes 4194304 | tf_op jit(solution)/shard_map/all_to_all | solution.py:37
Sparse Core Ops, SparseCore 0:
  9.5 230.2 all-gather.2
  285.3 56.4 all-gather.4
  427.1 71.7 reduce-scatter.1
where the time goes:
time: 616 us; the launch traced here: 614 us
  waiting for transfers between devices  361 us (59%)
  local copies, waits for them, and re-layouts  170 us (28%)
  matrix products  52.2 us (8%)
  between operations  13.2 us (2%)
  other arithmetic  12.5 us (2%)
    all_gather x1, waiting for transfers between devices, per_device(): gathered = lax.all_gather(amplitudes, 'wide', axis=0, tiled=True)  233 us
    reduce_scatter x1, waiting for transfers between devices, per_device(): lax.psum_scatter(terms.reshape(i_here * virt * lax.axis_size('narrow'), b...  71.9 us
    all_gather x1, waiting for transfers between devices, per_device(): every_k = lax.all_gather(mine, 'narrow', axis=2, tiled=True)  56.1 us
    gather x2, local copies, waits for them, and re-layouts, per_device(): picked = jnp.take(by_occupied, cycle_index, axis=0)  50.6 us
    dot_general x1, matrix products, per_device(): jnp.einsum('akbd,akdn->abn', ladder_blocks, taken, precision=lax.Precisio...  26.6 us
    unnamed x12, local copies, waits for them, and re-layouts  26 us
    dot_general x1, matrix products, per_device(): jnp.einsum('isac,iscn->ian', cycle_blocks, picked, precision=lax.Precisio...  25.6 us
    gather x1, local copies, waits for them, and re-layouts, per_device(): jnp.take(gathered.reshape(virt, virt, cols_here), ladder_index, axis=0)  20.7 us
  transfers between devices with their start and end apart: 4, of which 3 were waited for; matrix products, arithmetic and copies ran while one was open for 8% of the time, Pallas kernels for 0%

commit v1 on v0

v1 whole, which is shorter than its diff:
```python
import functools

import jax
import jax.numpy as jnp
from jax import lax
from jax.experimental import pallas as pl
from jax.experimental.pallas import tpu as pltpu
from jax.sharding import PartitionSpec as P

LANES = 128
PARTS = 4
F32 = jnp.float32
BF16 = jnp.bfloat16
ANY = pl.BlockSpec(memory_space=pl.ANY)
VMEM = pl.BlockSpec(memory_space=pltpu.VMEM)
SMEM = pl.BlockSpec(memory_space=pltpu.SMEM)


def params(mib, grid=0):
    semantics = ("arbitrary",) * grid if grid else None
    return pltpu.CompilerParams(vmem_limit_bytes=mib << 20, dimension_semantics=semantics)


def split(x):
    high = x.astype(BF16)
    return high, (x - high.astype(F32)).astype(BF16)


def dot(x, y):
    return jnp.dot(x, y, preferred_element_type=F32)


def swap_groups(arrays, group):
    arrays = list(arrays)
    count = len(arrays)
    lane = lax.broadcasted_iota(jnp.int32, arrays[0].shape, 1) // group
    bit = 1
    while bit < count:
        odd = (lane & bit) != 0
        for low in range(count):
            if low & bit:
                continue
            high = low | bit
            up = pltpu.roll(arrays[high], bit * group, 1)
            down = pltpu.roll(arrays[low], LANES - bit * group, 1)
            arrays[low], arrays[high] = (
                jnp.where(odd, up, arrays[low]),
                jnp.where(odd, arrays[high], down),
            )
        bit *= 2
    return arrays


def ladder_prep_kernel(blocks_ref, out_ref):
    slots, virt, _ = blocks_ref.shape[1:]
    parts = out_ref.shape[0]
    part = virt // parts
    per = LANES // part
    for first in range(0, slots, per):
        pieces = [blocks_ref[0, first + s] for s in range(per)]
        for q, piece in enumerate(swap_groups(pieces, part)):
            high, low = split(piece)
            lanes = pl.ds(first * part, LANES)
            out_ref[q, 0, 0:virt, lanes] = high
            out_ref[q, 0, virt : 2 * virt, lanes] = low


def ladder_prep(blocks, parts):
    a_here, slots, virt, _ = blocks.shape
    depth = slots * (virt // parts)
    return pl.pallas_call(
        ladder_prep_kernel,
        grid=(a_here,),
        in_specs=[pl.BlockSpec((1, slots, virt, virt), lambda a: (a, 0, 0, 0))],
        out_specs=pl.BlockSpec((parts, 1, 2 * virt, depth), lambda a: (0, a, 0, 0)),
        out_shape=jax.ShapeDtypeStruct((parts, a_here, 2 * virt, depth), BF16),
        compiler_params=params(24, 1),
        cost_estimate=pl.CostEstimate(
            flops=8 * blocks.size, bytes_accessed=8 * blocks.size, transcendentals=0
        ),
        name="ladder_prep",
    )(blocks)


def mirrored(rel, size):
    out = 0
    bit = 1
    while bit < size:
        out = out * 2 + (rel // bit) % 2
        bit *= 2
    return out


def cycle_prep_kernel(place_ref, index_ref, blocks_ref, high_ref, low_ref, dense):
    shares, occ, slots, a_here, virt = blocks_ref.shape
    i_here = occ // shares
    mine = place_ref[0]
    dense[...] = jnp.zeros_like(dense)
    for owner in range(shares):
        rel = mine ^ owner
        base = mirrored(rel, shares) * i_here

        @pl.loop(0, i_here)
        def _(i):
            for share in range(shares):
                for s in range(slots):
                    row = (share * occ + owner * i_here + i) * slots + s
                    k = index_ref[row] - mine * i_here

                    @pl.when((k >= 0) & (k < i_here))
                    def _():
                        lanes = pl.ds(pl.multiple_of(k * virt, virt), virt)
                        dense[base + i, :, lanes] = blocks_ref[share, owner * i_here + i, s]

    rows = occ * a_here
    step = i_here * a_here
    for first in range(shares):
        piece = dense[first * i_here : (first + 1) * i_here].reshape(step, i_here * virt)
        high, low = split(piece)
        high_ref[first * step : (first + 1) * step, :] = high
        low_ref[first * step : (first + 1) * step, :] = low


def cycle_prep(place, index, blocks):
    shares, occ, slots, a_here, virt = blocks.shape
    shape = jax.ShapeDtypeStruct((occ * a_here, occ // shares * virt), BF16)
    return pl.pallas_call(
        cycle_prep_kernel,
        in_specs=[SMEM, SMEM, VMEM],
        out_specs=[VMEM, VMEM],
        out_shape=[shape, shape],
        scratch_shapes=[pltpu.VMEM((occ, a_here, occ // shares * virt), F32)],
        compiler_params=params(24),
        cost_estimate=pl.CostEstimate(
            flops=2 * blocks.size, bytes_accessed=8 * blocks.size, transcendentals=0
        ),
        name="cycle_prep",
    )(place, index, blocks)


def fetch(source_ref, blocks, rows_each, held, sem):
    copies = []
    for n, (owner, offset, block) in enumerate(blocks):
        rows = block.shape[0]
        start = pl.multiple_of(source_ref[owner] * rows_each + offset, rows)
        for h in range(held.shape[0]):
            copies.append(
                pltpu.make_async_copy(
                    block.at[:, pl.ds(h * LANES, LANES)],
                    held.at[h, pl.ds(start, rows), :],
                    sem.at[n, h],
                )
            )
    for copy in copies:
        copy.start()
    return copies


def cycle_kernel(layout, part, occ, source_ref, *refs):
    count = len(layout)
    block_refs = refs[:count]
    high_ref, low_ref, keep_ref, send_ref, held, cols_high, cols_low, sem = refs[count:]
    halves, rows, _ = held.shape
    virt = rows // part
    rows_each = sum(n for o, _, n in layout if o == 0)
    blocks = [(o, f, r) for (o, f, _), r in zip(layout, block_refs)]
    for copy in fetch(source_ref, blocks, rows_each, held, sem):
        copy.wait()
    per = LANES // occ
    half_rows = keep_ref.shape[0]
    width = 2 * LANES
    steps = part // per

    for first in range(0, steps, 2):
        for g in range(first, first + 2):
            for h in range(halves):
                pieces = [held[h, pl.ds(g * per + m, virt, stride=part), :] for m in range(per)]
                for m, piece in enumerate(swap_groups(pieces, occ)):
                    k = h * per + m
                    high, low = split(piece)
                    lanes = pl.ds(g * LANES, LANES)
                    cols_high[k * virt : (k + 1) * virt, lanes] = high
                    cols_low[k * virt : (k + 1) * virt, lanes] = low
        lanes = pl.ds(first * LANES, width)
        right_high = cols_high[:, lanes]
        right_low = cols_low[:, lanes]
        for out_ref, top in ((send_ref, half_rows), (keep_ref, 0)):
            left_high = high_ref[top : top + half_rows, :]
            left_low = low_ref[top : top + half_rows, :]
            out_ref[:, lanes] = (
                dot(left_high, right_high) + dot(left_low, right_high) + dot(left_high, right_low)
            )


def cycle_part(layout, part, virt, occ, source, blocks, high, low):
    cols = blocks[0].shape[1]
    halves = cols // LANES
    rows, depth = high.shape
    wide = part * occ
    shape = jax.ShapeDtypeStruct((rows // 2, wide), F32)
    return pl.pallas_call(
        functools.partial(cycle_kernel, layout, part, occ),
        in_specs=[SMEM] + [ANY] * len(blocks) + [VMEM, VMEM],
        out_specs=[VMEM, VMEM],
        out_shape=[shape, shape],
        scratch_shapes=[
            pltpu.VMEM((halves, virt * part, LANES), F32),
            pltpu.VMEM((depth, wide), BF16),
            pltpu.VMEM((depth, wide), BF16),
            pltpu.SemaphoreType.DMA((len(blocks), halves)),
        ],
        compiler_params=params(40),
        cost_estimate=pl.CostEstimate(
            flops=6 * rows * depth * wide, bytes_accessed=4 * virt * part * cols, transcendentals=0
        ),
        name="cycle_part",
    )(source, *blocks, high, low)


def ladder_kernel(layout, part, again, source_ref, index_ref, *refs):
    count = len(layout)
    block_refs = refs[:count]
    left_ref = refs[count]
    before_ref = refs[count + 1] if again else None
    out_ref, held, right_high, right_low, sem = refs[count + 1 + again :]
    halves = held.shape[0]
    virt = out_ref.shape[1]
    slots = right_high.shape[0] // part
    a = pl.program_id(0)
    rows_each = sum(n for o, _, n in layout if o == 0)
    blocks = [(o, f, r) for (o, f, _), r in zip(layout, block_refs)]

    @pl.when(a == 0)
    def _():
        for copy in fetch(source_ref, blocks, rows_each, held, sem):
            copy.wait()

    for s in range(slots):
        start = pl.multiple_of(index_ref[a * slots + s] * part, part)
        for h in range(halves):
            high, low = split(held[h, pl.ds(start, part), :])
            right_high[s * part : (s + 1) * part, h * LANES : (h + 1) * LANES] = high
            right_low[s * part : (s + 1) * part, h * LANES : (h + 1) * LANES] = low
    both = dot(left_ref[0, 0], right_high[...])
    total = both[:virt] + both[virt:] + dot(left_ref[0, 0, :virt], right_low[...])
    if again:
        total = total + before_ref[0]
    out_ref[0] = total


def ladder_part(layout, part, q, source, index, blocks, left, before):
    cols = blocks[0].shape[1]
    halves = cols // LANES
    _, a_here, rows, depth = left.shape
    virt = rows // 2
    again = before is not None
    spec = pl.BlockSpec((1, virt, cols), lambda a, *_: (a, 0, 0))
    grid_spec = pltpu.PrefetchScalarGridSpec(
        num_scalar_prefetch=2,
        grid=(a_here,),
        in_specs=[ANY] * len(blocks)
        + [pl.BlockSpec((1, 1, rows, depth), lambda a, *_: (q, a, 0, 0))]
        + [spec] * again,
        out_specs=spec,
        scratch_shapes=[
            pltpu.VMEM((halves, virt * part, LANES), F32),
            pltpu.VMEM((depth, cols), BF16),
            pltpu.VMEM((depth, cols), BF16),
            pltpu.SemaphoreType.DMA((len(blocks), halves)),
        ],
    )
    aliases = {3 + len(blocks): 0} if again else {}
    return pl.pallas_call(
        functools.partial(ladder_kernel, layout, part, again),
        grid_spec=grid_spec,
        out_shape=jax.ShapeDtypeStruct((a_here, virt, cols), F32),
        input_output_aliases=aliases,
        compiler_params=params(24, 1),
        cost_estimate=pl.CostEstimate(
            flops=3 * a_here * rows * depth * cols,
            bytes_accessed=2 * left.size // left.shape[0],
            transcendentals=0,
        ),
        name="ladder_part",
    )(source, index, *blocks, left, *([before] if again else []))


def finish_kernel(parts, part, occ, virt_ref, *refs):
    energy_a, energy_ij, ladder_ref = refs[:3]
    terms = refs[3 : 3 + 3 * parts]
    out_ref = refs[3 + 3 * parts]
    a_here = energy_a.shape[0]
    halves, rows, _ = ladder_ref.shape
    virt = rows // a_here
    per = LANES // occ
    for q in range(parts):
        keep_ref, near_ref, far_ref = terms[3 * q : 3 * q + 3]

        @pl.loop(0, part // per)
        def _(g):
            lanes = pl.ds(pl.multiple_of(g * LANES, LANES), LANES)
            for h in range(halves):
                pieces = []
                for m in range(per):
                    here = pl.ds((h * per + m) * a_here, a_here)
                    pieces.append(keep_ref[here, lanes] + near_ref[here, lanes] + far_ref[here, lanes])
                for m, piece in enumerate(swap_groups(pieces, occ)):
                    b = q * part + g * per + m
                    here = pl.ds(b, a_here, stride=virt)
                    low = energy_a[...] + virt_ref[b] - energy_ij[h : h + 1, :]
                    out_ref[h, here, :] = (ladder_ref[h, here, :] + piece) / low


def finish(eps_virt, energy_a, energy_ij, ladder, terms, parts, part, occ):
    return None


def finish_body(parts, part, occ, virt_ref, energy_a, energy_ij, ladder_hbm, *refs):
    terms = refs[: 3 * parts]
    out_hbm, ladder_ref, out_ref, sem = refs[3 * parts :]
    halves = ladder_ref.shape[0]
    copies = [
        pltpu.make_async_copy(
            ladder_hbm.at[:, pl.ds(h * LANES, LANES)], ladder_ref.at[h], sem.at[h]
        )
        for h in range(halves)
    ]
    for copy in copies:
        copy.start()
    for copy in copies:
        copy.wait()
    finish_kernel(parts, part, occ, virt_ref, energy_a, energy_ij, ladder_ref, *terms, out_ref)
    copies = [
        pltpu.make_async_copy(out_ref.at[h], out_hbm.at[:, pl.ds(h * LANES, LANES)], sem.at[h])
        for h in range(halves)
    ]
    for copy in copies:
        copy.start()
    for copy in copies:
        copy.wait()


def finish_call(eps_virt, energy_a, energy_ij, ladder, terms, parts, part, occ):
    rows, cols = ladder.shape
    halves = cols // LANES
    return pl.pallas_call(
        functools.partial(finish_body, parts, part, occ),
        in_specs=[SMEM, VMEM, VMEM, ANY] + [VMEM] * len(terms),
        out_specs=ANY,
        out_shape=jax.ShapeDtypeStruct((rows, cols), F32),
        scratch_shapes=[
            pltpu.VMEM((halves, rows, LANES), F32),
            pltpu.VMEM((halves, rows, LANES), F32),
            pltpu.SemaphoreType.DMA((halves,)),
        ],
        compiler_params=params(32),
        name="finish",
    )(eps_virt, energy_a, energy_ij, ladder, *terms)


def ring_order(size):
    return list(range(0, size, 2)) + list(range(size - 1 - size % 2, 0, -2))


def per_device(
    amplitudes, ladder_blocks, ladder_index, cycle_blocks, cycle_index, eps_virt, eps_occ
):
    virt = eps_virt.shape[0]
    occ = eps_occ.shape[0]
    rows_here, cols = amplitudes.shape
    a_here = rows_here // virt
    i_here = cols // occ
    wide = lax.axis_size("wide")
    narrow = lax.axis_size("narrow")
    wide_pos = lax.axis_index("wide")
    narrow_pos = lax.axis_index("narrow")
    parts = PARTS
    part = virt // parts

    order = ring_order(wide)
    ahead = [(order[r], order[(r + 1) % wide]) for r in range(wide)]
    back = [(order[(r + 1) % wide], order[r]) for r in range(wide)]
    order_now = jnp.asarray(order, jnp.int32)
    spot = jnp.asarray([order.index(w) for w in range(wide)], jnp.int32)[wide_pos]
    steps = (wide - 1) // 2
    shifts = [0]
    for s in range(1, steps + 1):
        shifts += [-s, s]
    if wide % 2 == 0:
        shifts.append(wide // 2)
    source = order_now[(spot + jnp.asarray(shifts, jnp.int32)) % wide]

    own = amplitudes.reshape(a_here, virt, cols)
    rows_each = a_here * part

    place = narrow_pos.reshape(1).astype(jnp.int32)
    picked = lax.dynamic_slice_in_dim(cycle_blocks, wide_pos * a_here, a_here, 2)
    cycle_all = lax.all_gather(picked, "narrow", axis=0)
    index_all = lax.all_gather(cycle_index, "narrow", axis=0).reshape(-1)

    layout = None
    gathered = []
    for q in range(parts):
        block = own[:, q * part : (q + 1) * part, :].reshape(rows_each, cols)
        if q >= 2:
            block, _ = lax.optimization_barrier((block, gathered[q - 2][-3]))
        blocks = [block]
        layout = [(0, 0, rows_each)]
        right = left = block
        for s in range(steps):
            right = lax.ppermute(right, "wide", ahead)
            left = lax.ppermute(left, "wide", back)
            blocks += [right, left]
            layout += [(2 * s + 1, 0, rows_each), (2 * s + 2, 0, rows_each)]
        if wide % 2 == 0:
            half = rows_each // 2
            blocks.append(lax.ppermute(right[:half], "wide", ahead))
            blocks.append(lax.ppermute(left[half:], "wide", back))
            layout += [(wide - 1, 0, half), (wide - 1, half, rows_each - half)]
        gathered.append(blocks)

    left_all = ladder_prep(ladder_blocks, parts)
    dense_high, dense_low = cycle_prep(place, index_all, cycle_all)

    ladder = None
    terms = []
    ladder_list = ladder_index.reshape(-1)
    for q in range(parts):
        keep, send = cycle_part(layout, part, virt, occ, source, gathered[q], dense_high, dense_low)
        rows = keep.shape[0]
        near = lax.ppermute(send, "narrow", [(n, n ^ 1) for n in range(narrow)])
        pass_on = keep[rows // 2 :] + near[rows // 2 :]
        far = lax.ppermute(pass_on, "narrow", [(n, n ^ 2) for n in range(narrow)])
        terms += [keep, near, far]
        ladder = ladder_part(layout, part, q, source, ladder_list, gathered[q], left_all, ladder)

    energy_a = lax.dynamic_slice_in_dim(eps_virt, wide_pos * a_here, a_here, 0)
    energy_i = lax.dynamic_slice_in_dim(eps_occ, narrow_pos * i_here, i_here, 0)
    energy_ij = (energy_i[:, None] + eps_occ[None, :]).reshape(cols // LANES, LANES)
    energy_a = jnp.broadcast_to(energy_a[:, None], (a_here, LANES))
    return finish_call(
        eps_virt, energy_a, energy_ij, ladder.reshape(rows_here, cols), terms, parts, part, occ
    )


def solution(mesh):
    in_specs = (
        P("wide", "narrow"),
        P("wide", None, None, None),
        P("wide", None),
        P(None, "narrow", None, None),
        P(None, "narrow"),
        P(),
        P(),
    )
    out_specs = P("wide", "narrow")
    return jax.shard_map(
        per_device, mesh=mesh, in_specs=in_specs, out_specs=out_specs, check_vma=False
    )
```

time: 616 us -> 323 us (0.52)
  waiting for transfers between devices: 361 us -> 120 us
  local copies, waits for them, and re-layouts: 170 us -> 34.7 us
  Pallas kernels: 0 us -> 99.3 us
  matrix products: 52.2 us -> 0 us
  starting transfers between devices: 5.77 us -> 42.5 us
  other arithmetic: 12.5 us -> 5.34 us
    all_gather x2 -> x1, waiting for transfers between devices: 289 us -> 0.01 us  [per_device(): cycle_all = lax.all_gather(picked, 'narrow', axis=0)]
    ppermute x0 -> x40, waiting for transfers between devices: none -> 120 us  [the longest x12 64.4 us: per_device(): right = lax.ppermute(right, 'wide', ahead)]
    pallas_call x0 -> x11, Pallas kernels: none -> 99.3 us  [the longest x4 34.4 us: cycle_part(): pl.pallas_call(functools.partial(cycle_kernel, layout, part, occ), in_spe...]
    reduce_scatter x1 -> x0, waiting for transfers between devices: 71.9 us -> none  [per_device(): lax.psum_scatter(terms.reshape(i_here * virt * lax.axis_size('narrow'), b...]
    gather x3 -> x1, local copies, waits for them, and re-layouts: 71.4 us -> 0.64 us  [per_device(): source = order_now[(spot + jnp.asarray(shifts, jnp.int32)) % wide]]
    dot_general x2 -> x0, matrix products: 52.2 us -> none  [the longest x1 26.6 us: per_device(): jnp.einsum('akbd,akdn->abn', ladder_blocks, taken, precision=lax.Precisio...]
    ppermute x0 -> x40, starting transfers between devices: none -> 42.5 us  [the longest x12 20.2 us: per_device(): left = lax.ppermute(left, 'wide', back)]
    reshape x3 -> x2, local copies, waits for them, and re-layouts: 18.9 us -> 0.19 us  [the longest x1 0.11 us: per_device(): index_all = lax.all_gather(cycle_index, 'narrow', axis=0).reshape(-1)]
  transfers between devices with their start and end apart: 4 -> 41, of which waited for: 3 -> 16; matrix products, arithmetic and copies ran while one was open for 8% -> 6% of each run, Pallas kernels for 0% -> 28%
where the time goes in v1:
time: 323 us; the launch traced here: 322 us
  waiting for transfers between devices  120 us (37%)
  Pallas kernels  99.3 us (31%)
  starting transfers between devices  42.5 us (13%)
  local copies, waits for them, and re-layouts  34.7 us (11%)
  between operations  14.2 us (4%)
  other arithmetic  5.34 us (2%)
  blocking collectives  5.15 us (2%)
    ppermute x12, waiting for transfers between devices, per_device(): right = lax.ppermute(right, 'wide', ahead)  64.4 us
    ppermute x12, waiting for transfers between devices, per_device(): left = lax.ppermute(left, 'wide', back)  48.4 us
    pallas_call x4, Pallas kernels, cycle_part(): pl.pallas_call(functools.partial(cycle_kernel, layout, part, occ), in_spe...  34.4 us
    pallas_call x4, Pallas kernels, ladder_part(): pl.pallas_call(functools.partial(ladder_kernel, layout, part, again), gri...  30.6 us
    ppermute x12, starting transfers between devices, per_device(): left = lax.ppermute(left, 'wide', back)  20.2 us
    pallas_call x1, Pallas kernels, ladder_prep(): pl.pallas_call(ladder_prep_kernel, grid=(a_here,), in_specs=[pl.BlockSpec...  17.7 us
    unnamed x136, local copies, waits for them, and re-layouts  17 us
    pallas_call x1, Pallas kernels, finish_call(): pl.pallas_call(functools.partial(finish_body, parts, part, occ), in_specs...  10.2 us
  transfers between devices with their start and end apart: 41, of which 16 were waited for; matrix products, arithmetic and copies ran while one was open for 6% of the time, Pallas kernels for 28%

profile of v1, /device:TPU:0, one launch (start us, length us, event | category | flops | bytes accessed | tf_op | source)
XLA Modules:
  0.0 321.7 jit_solution(3119452261326113637)
XLA Ops:
  6.5 2.3 constant_dynamic-slice_fusion
  8.9 1.7 fusion.1
  10.7 3.0 collective-permute-start
  13.7 1.6 collective-permute-start.11
  15.3 11.3 %collective-permute-done.refs_2_ = f32[512,256]{1,0:T(8,128)S(1)} collective-permute-done((f32[512,256]{1,0:T(8,128)S(1)}, f32[512,256]{1,0:T(8,128)S(1)}, u32[]{:S(2)}, u32[]{:S(2)}) %collective-permute-start) | collective-permute-done | bytes 524320 | tf_op jit(solution)/shard_map/ppermute | solution.py:412
  26.5 2.0 collective-permute-start.1
  29.3 8.5 %collective-permute-done.11.refs_2_ = f32[512,256]{1,0:T(8,128)S(1)} collective-permute-done((f32[512,256]{1,0:T(8,128)S(1)}, f32[512,256]{1,0:T(8,128)S(1)}, u32[]{:S(2)}, u32[]{:S(2)}) %collective-permute-start.11) | collective-permute-done | bytes 524320 | tf_op jit(solution)/shard_map/ppermute | solution.py:412
  37.8 2.0 collective-permute-start.12
  40.7 2.0 collective-permute-start.27
  42.7 6.3 %collective-permute-done.1.refs_4_ = f32[512,256]{1,0:T(8,128)S(1)} collective-permute-done((f32[512,256]{1,0:T(8,128)S(1)}, f32[512,256]{1,0:T(8,128)S(1)}, u32[]{:S(2)}, u32[]{:S(2)}) %collective-permute-start.1) | collective-permute-done | bytes 524320 | tf_op jit(solution)/shard_map/ppermute | solution.py:412
  49.0 2.0 collective-permute-start.2
  51.8 8.5 %collective-permute-done.12.refs_4_ = f32[512,256]{1,0:T(8,128)S(1)} collective-permute-done((f32[512,256]{1,0:T(8,128)S(1)}, f32[512,256]{1,0:T(8,128)S(1)}, u32[]{:S(2)}, u32[]{:S(2)}) %collective-permute-start.12) | collective-permute-done | bytes 524320 | tf_op jit(solution)/shard_map/ppermute | solution.py:412
  60.3 2.0 collective-permute-start.13
  63.9 2.0 collective-permute-start.28
  66.8 4.7 %collective-permute-done.2.refs_6_ = f32[512,256]{1,0:T(8,128)S(1)} collective-permute-done((f32[512,256]{1,0:T(8,128)S(1)}, f32[512,256]{1,0:T(8,128)S(1)}, u32[]{:S(2)}, u32[]{:S(2)}) %collective-permute-start.2) | collective-permute-done | bytes 524320 | tf_op jit(solution)/shard_map/ppermute | solution.py:412
  71.5 2.1 collective-permute-start.3
  73.6 9.2 %collective-permute-done.13.refs_6_ = f32[512,256]{1,0:T(8,128)S(1)} collective-permute-done((f32[512,256]{1,0:T(8,128)S(1)}, f32[512,256]{1,0:T(8,128)S(1)}, u32[]{:S(2)}, u32[]{:S(2)}) %collective-permute-start.13) | collective-permute-done | bytes 524320 | tf_op jit(solution)/shard_map/ppermute | solution.py:412
  82.7 2.1 collective-permute-start.14
  84.8 4.3 %collective-permute-done.28.refs_3_ = f32[512,256]{1,0:T(8,128)S(1)} collective-permute-done((f32[512,256]{1,0:T(8,128)S(1)}, f32[512,256]{1,0:T(8,128)S(1)}, u32[]{:S(2)}, u32[]{:S(2)}) %collective-permute-start.28) | collective-permute-done | bytes 524320 | tf_op jit(solution)/shard_map/ppermute | solution.py:411
  90.1 10.3 %collective-permute-done.3.refs_1_ = f32[512,256]{1,0:T(8,128)S(1)} collective-permute-done((f32[512,256]{1,0:T(8,128)S(1)}, f32[512,256]{1,0:T(8,128)S(1)}, u32[]{:S(2)}, u32[]{:S(2)}) %collective-permute-start.3) | collective-permute-done | bytes 524320 | tf_op jit(solution)/shard_map/ppermute | solution.py:411
  101.3 1.9 collective-permute-start.6
  104.0 7.6 %collective-permute-done.14.refs_1_ = f32[512,256]{1,0:T(8,128)S(1)} collective-permute-done((f32[512,256]{1,0:T(8,128)S(1)}, f32[512,256]{1,0:T(8,128)S(1)}, u32[]{:S(2)}, u32[]{:S(2)}) %collective-permute-start.14) | collective-permute-done | bytes 524320 | tf_op jit(solution)/shard_map/ppermute | solution.py:411
  112.5 1.9 collective-permute-start.17
  115.2 7.7 %collective-permute-done.29.refs_5_ = f32[512,256]{1,0:T(8,128)} collective-permute-done((f32[512,256]{1,0:T(8,128)S(1)}, f32[512,256]{1,0:T(8,128)}, u32[]{:S(2)}, u32[]{:S(2)}) %collective-permute-start.29) | collective-permute-done | bytes 524320 | tf_op jit(solution)/shard_map/ppermute | solution.py:411
  123.0 11.1 %collective-permute-done.5.refs_3_ = f32[512,256]{1,0:T(8,128)} collective-permute-done((f32[512,256]{1,0:T(8,128)S(1)}, f32[512,256]{1,0:T(8,128)}, u32[]{:S(2)}, u32[]{:S(2)}) %collective-permute-start.5) | collective-permute-done | bytes 524320 | tf_op jit(solution)/shard_map/ppermute | solution.py:411
  134.3 1.9 collective-permute-start.8
  136.2 9.2 %collective-permute-done.16.refs_3_ = f32[512,256]{1,0:T(8,128)} collective-permute-done((f32[512,256]{1,0:T(8,128)S(1)}, f32[512,256]{1,0:T(8,128)}, u32[]{:S(2)}, u32[]{:S(2)}) %collective-permute-start.16) | collective-permute-done | bytes 524320 | tf_op jit(solution)/shard_map/ppermute | solution.py:411
  145.5 1.9 collective-permute-start.19
  147.4 5.2 %all-gather.2 = s32[4,32,4]{1,2,0:T(4,128)S(1)} all-gather(s32[1,32,4]{1,2,0:T(4,128)S(1)} %bitcast.29), channel_id=2, replica_groups=mesh['wide'=8,'narrow'=4] {'narrow'}, dimensions={0}, use_global_device_ids=true | all-gather | bytes 2560 | tf_op jit(solution)/shard_map/all_gather | solution.py:399
  154.2 1.7 slice.92
  156.7 11.1 %collective-permute-done.7.refs_5_ = f32[512,256]{1,0:T(8,128)} collective-permute-done((f32[512,256]{1,0:T(8,128)}, f32[512,256]{1,0:T(8,128)}, u32[]{:S(2)}, u32[]{:S(2)}) %collective-permute-start.7) | collective-permute-done | bytes 524320 | tf_op jit(solution)/shard_map/ppermute | solution.py:411
  167.9 1.6 collective-permute-start.31
  171.5 1.7 slice.90
  173.2 1.7 slice.84
  175.3 1.7 slice.85
  177.0 2.1 collective-permute-done.18.refs_5_
  179.1 1.6 collective-permute-start.26
  180.7 1.7 slice.88
  182.9 1.7 slice.89
  184.5 2.2 copy-done.2
  186.8 6.4 %cycle_prep.1 = (bf16[512,1024]{1,0:T(8,128)(2,1)S(1)}, bf16[512,1024]{1,0:T(8,128)(2,1)S(1)}) custom-call(s32[1]{0:T(128)} %bitcast.7.place_ref, s32[512]{0:T(512)S(1)} %reshape.43.index_ref, f32[4,32,4,16,128]{4,3,2,1,0:T(8,128)S(1)} %bitcast.11), custom_call_target="tpu_custom_call" | custom-call | flops 2097152 | bytes 8388608 | tf_op jit(solution)/shard_map/cycle_prep/pallas_call | solution.py:127
  193.2 1.6 collective-permute-start.10
  195.4 8.4 %cycle_part.4 = (f32[256,1024]{1,0:T(8,128)S(1)}, f32[256,1024]{1,0:T(8,128)}) custom-call(s32[8]{0:T(128)S(1)} %gather_fusion, f32[512,256]{1,0:T(8,128)S(1)} %bitcast.26, f32[512,256]{1,0:T(8,128)S(1)} %copy-done.35, f32[512,256]{1,0:T(8,128)S(1)} %copy-done.26, f32[512,256]{1,0:T(8,128)S(1)} %copy-done.44, f32[512,256]{1,0:T(8,128)S(1)} %copy-done.32, ...), custom_call_target="tpu_custom_call" | custom-call | flops 3221225472 | bytes 4194304 | tf_op jit(solution)/shard_map/cycle_part/pallas_call | solution.py:201
  203.8 1.8 collective-permute-start.21
  205.6 8.5 %cycle_part.5 = (f32[256,1024]{1,0:T(8,128)S(1)}, f32[256,1024]{1,0:T(8,128)}) custom-call(s32[8]{0:T(128)S(1)} %gather_fusion, f32[512,256]{1,0:T(8,128)S(1)} %bitcast.22, f32[512,256]{1,0:T(8,128)S(1)} %copy-done.29, f32[512,256]{1,0:T(8,128)S(1)} %copy-done.20, f32[512,256]{1,0:T(8,128)} %collective-permute-done.23.refs_3_, f32[512,256]{1,0:T(8,128)S(1)} %copy-done.23, ...), custom_call_target="tpu_custom_call" | custom-call | flops 3221225472 | bytes 4194304 | tf_op jit(solution)/shard_map/cycle_part/pallas_call | solution.py:201
  214.2 1.0 copy-done.3
  215.7 8.7 %cycle_part.6 = (f32[256,1024]{1,0:T(8,128)S(1)}, f32[256,1024]{1,0:T(8,128)}) custom-call(s32[8]{0:T(128)S(1)} %gather_fusion, f32[512,256]{1,0:T(8,128)S(1)} %bitcast.18, f32[512,256]{1,0:T(8,128)S(1)} %copy-done.47, f32[512,256]{1,0:T(8,128)S(1)} %copy-done.50, f32[512,256]{1,0:T(8,128)} %collective-permute-done.16.refs_3_, ...), custom_call_target="tpu_custom_call" | custom-call | flops 3221225472 | bytes 4194304 | tf_op jit(solution)/shard_map/cycle_part/pallas_call | solution.py:201
  224.5 0.9 copy-done.5
  225.6 8.7 %cycle_part.7 = (f32[256,1024]{1,0:T(8,128)S(1)}, f32[256,1024]{1,0:T(8,128)}) custom-call(s32[8]{0:T(128)S(1)} %gather_fusion, f32[512,256]{1,0:T(8,128)S(1)} %bitcast.14, f32[512,256]{1,0:T(8,128)S(1)} %copy-done.38, f32[512,256]{1,0:T(8,128)S(1)} %copy-done.41, f32[512,256]{1,0:T(8,128)} %collective-permute-done.5.refs_3_, ...), custom_call_target="tpu_custom_call" | custom-call | flops 3221225472 | bytes 4194304 | tf_op jit(solution)/shard_map/cycle_part/pallas_call | solution.py:201
  236.3 17.7 %ladder_prep.1.refs_9_ = bf16[4,16,256,512]{3,2,1,0:T(8,128)(2,1)S(1)} custom-call(f32[16,16,128,128]{3,2,1,0:T(8,128)} %blocks_ref.1), custom_call_target="tpu_custom_call" | custom-call | flops 33554432 | bytes 33554432 | tf_op jit(solution)/shard_map/ladder_prep/pallas_call | solution.py:71
  254.1 1.2 slice_add_fusion.3
  255.3 1.6 collective-permute-start.33
  257.0 1.3 slice_add_fusion.2
  258.8 1.1 slice_add_fusion.1
  259.9 1.6 collective-permute-start.37
  261.5 1.1 slice_add_fusion
  263.2 7.4 %ladder_part.4.refs_10_ = f32[16,128,256]{2,1,0:T(8,128)S(1)} custom-call(s32[8]{0:T(128)S(1)} %gather_fusion, s32[256]{0:T(256)S(1)} %reshape.35.index_ref, f32[512,256]{1,0:T(8,128)S(1)} %bitcast.27, f32[512,256]{1,0:T(8,128)S(1)} %copy-done.36, f32[512,256]{1,0:T(8,128)S(1)} %copy-done.27, f32[512,256]{1,0:T(8,128)S(1)} %copy-done.45, ...), custom_call_target="tpu_custom_call" | custom-call | flops 1610612736 | bytes 4194304 | tf_op jit(solution)/shard_map/ladder_part/pallas_call | solution.py:273
  270.8 7.6 %ladder_part.5.refs_10_ = f32[16,128,256]{2,1,0:T(8,128)S(1)} custom-call(s32[8]{0:T(128)S(1)} %gather_fusion, s32[256]{0:T(256)S(1)} %reshape.35.index_ref, f32[512,256]{1,0:T(8,128)S(1)} %bitcast.23, f32[512,256]{1,0:T(8,128)S(1)} %copy-done.30, f32[512,256]{1,0:T(8,128)S(1)} %copy-done.21, ...), custom_call_target="tpu_custom_call", output_to_operand_aliasing={{}: (12, {})} | custom-call | flops 1610612736 | bytes 4194304 | tf_op jit(solution)/shard_map/ladder_part/pallas_call | solution.py:273
  278.5 7.8 %ladder_part.6.refs_10_ = f32[16,128,256]{2,1,0:T(8,128)S(1)} custom-call(s32[8]{0:T(128)S(1)} %gather_fusion, s32[256]{0:T(256)S(1)} %reshape.35.index_ref, f32[512,256]{1,0:T(8,128)S(1)} %bitcast.19, f32[512,256]{1,0:T(8,128)S(1)} %copy-done.48, f32[512,256]{1,0:T(8,128)S(1)} %copy-done.51, ...), custom_call_target="tpu_custom_call", output_to_operand_aliasing={{}: (12, {})} | custom-call | flops 1610612736 | bytes 4194304 | tf_op jit(solution)/shard_map/ladder_part/pallas_call | solution.py:273
  286.3 7.8 %ladder_part.7 = f32[16,128,256]{2,1,0:T(8,128)S(1)} custom-call(s32[8]{0:T(128)S(1)} %gather_fusion, s32[256]{0:T(256)S(1)} %reshape.35.index_ref, f32[512,256]{1,0:T(8,128)S(1)} %bitcast.15, f32[512,256]{1,0:T(8,128)S(1)} %copy-done.39, f32[512,256]{1,0:T(8,128)S(1)} %copy-done.42, ...), custom_call_target="tpu_custom_call", output_to_operand_aliasing={{}: (12, {})} | custom-call | flops 1610612736 | bytes 4194304 | tf_op jit(solution)/shard_map/ladder_part/pallas_call | solution.py:273
  294.1 1.3 copy-done
  295.4 7.6 %collective-permute-done.39.refs_11_ = f32[128,1024]{1,0:T(8,128)S(1)} collective-permute-done((f32[128,1024]{1,0:T(8,128)S(1)}, f32[128,1024]{1,0:T(8,128)S(1)}, u32[]{:S(2)}, u32[]{:S(2)}) %collective-permute-start.39) | collective-permute-done | bytes 524320 | tf_op jit(solution)/shard_map/ppermute | solution.py:433
  303.0 1.6 copy-done.1
  304.6 10.2 %finish.1 = f32[2048,256]{1,0:T(8,128)} custom-call(f32[128]{0:T(128)S(1)} %copy-done.58, f32[16,128]{1,0:T(8,128)S(1)} %broadcast_in_dim.4.energy_a, f32[2,128]{1,0:T(2,128)S(1)} %broadcast_add_fusion.energy_ij, f32[2048,256]{1,0:T(8,128)S(1)} %bitcast.10, f32[256,1024]{1,0:T(8,128)S(1)} %get-tuple-element.21.refs_0_, ...), custom_call_target="tpu_custom_call" | custom-call | tf_op jit(solution)/shard_map/finish/pallas_call | solution.py:346
  (197 shorter events, 19.6 us)
Async XLA Ops:
  6.5 178.0 %all-gather.5.cloned.1.call-start = ((), (), s32[]{:S(2)}) async-start(), calls=%async_computation | async-start | bytes 5242880 | tf_op jit(solution)/shard_map/all_gather | solution.py:398
  8.9 138.6 %copy-start.64 = (s32[32,4]{0,1:T(4,128)S(1)}, s32[32,4]{0,1:T(4,128)}, u32[]{:S(2)}) copy-start(s32[32,4]{0,1:T(4,128)} %param.14) | copy-start | bytes 1540
  8.9 143.9 %copy-start.67 = (s32[8]{0:T(128)S(1)}, s32[8]{0:T(128)}, u32[]{:S(2)}) copy-start(s32[8]{0:T(128)} %constant.40.clone) | copy-start | bytes 100
  8.9 160.5 %copy-start.66 = (s32[8]{0:T(128)S(1)}, s32[8]{0:T(128)}, u32[]{:S(2)}) copy-start(s32[8]{0:T(128)} %constant.41.clone) | copy-start | bytes 100
  8.9 161.2 %copy-start.59 = (s32[8]{0:T(128)S(1)}, s32[8]{0:T(128)}, u32[]{:S(2)}) copy-start(s32[8]{0:T(128)} %constant.39.clone) | copy-start | bytes 100
  10.7 171.7 %copy-start.13 = (f32[16,32,256]{2,1,0:T(8,128)}, f32[16,32,256]{2,1,0:T(8,128)S(1)}, u32[]{:S(2)}) copy-start(f32[16,32,256]{2,1,0:T(8,128)S(1)} %get-tuple-element.29) | copy-start | bytes 1572868
  10.7 194.9 %copy-start.11 = (f32[16,32,256]{2,1,0:T(8,128)}, f32[16,32,256]{2,1,0:T(8,128)S(1)}, u32[]{:S(2)}) copy-start(f32[16,32,256]{2,1,0:T(8,128)S(1)} %get-tuple-element.31) | copy-start | bytes 1572868
  10.7 205.0 %copy-start.9 = (f32[16,32,256]{2,1,0:T(8,128)}, f32[16,32,256]{2,1,0:T(8,128)S(1)}, u32[]{:S(2)}) copy-start(f32[16,32,256]{2,1,0:T(8,128)S(1)} %get-tuple-element.30) | copy-start | bytes 1572868
  10.7 15.8 %collective-permute-start = (f32[512,256]{1,0:T(8,128)S(1)}, f32[512,256]{1,0:T(8,128)S(1)}, u32[]{:S(2)}, u32[]{:S(2)}) collective-permute-start(f32[512,256]{1,0:T(8,128)S(1)} %bitcast.20), channel_id=1, source_target_pairs={{8,0},{16,8},{24,16},{28,24},{20,28},{12,20},{4,12},{0,4},{9,1},{1... | collective-permute-start | bytes 1572872 | tf_op jit(solution)/shard_map/ppermute | solution.py:412
  13.7 24.1 %collective-permute-start.11 = (f32[512,256]{1,0:T(8,128)S(1)}, f32[512,256]{1,0:T(8,128)S(1)}, u32[]{:S(2)}, u32[]{:S(2)}) collective-permute-start(f32[512,256]{1,0:T(8,128)S(1)} %bitcast.24), channel_id=1, source_target_pairs={{8,0},{16,8},{24,16},{28,24},{20,28},{12,20},{4,12},{0,4},{9,1},{1... | collective-permute-start | bytes 1572872 | tf_op jit(solution)/shard_map/ppermute | solution.py:412
  26.5 22.5 %collective-permute-start.1 = (f32[512,256]{1,0:T(8,128)S(1)}, f32[512,256]{1,0:T(8,128)S(1)}, u32[]{:S(2)}, u32[]{:S(2)}) collective-permute-start(f32[512,256]{1,0:T(8,128)S(1)} %collective-permute-done.refs_2_), channel_id=1, source_target_pairs={{8,0},{16,8},{24,16},{28,24},{20,28},{12,20},{4,12},{0,4},{9,1},{1... | collective-permute-start | bytes 1572872 | tf_op jit(solution)/shard_map/ppermute | solution.py:412
  37.8 22.5 %collective-permute-start.12 = (f32[512,256]{1,0:T(8,128)S(1)}, f32[512,256]{1,0:T(8,128)S(1)}, u32[]{:S(2)}, u32[]{:S(2)}) collective-permute-start(f32[512,256]{1,0:T(8,128)S(1)} %collective-permute-done.11.refs_2_), channel_id=1, source_target_pairs={{8,0},{16,8},{24,16},{28,24},{20,28},{12,20},{4,12},{0,4},{9,1},{1... | collective-permute-start | bytes 1572872 | tf_op jit(solution)/shard_map/ppermute | solution.py:412
  40.6 22.5 %collective-permute-start.22 = (f32[512,256]{1,0:T(8,128)S(1)}, f32[512,256]{1,0:T(8,128)S(1)}, u32[]{:S(2)}, u32[]{:S(2)}) collective-permute-start(f32[512,256]{1,0:T(8,128)S(1)} %bitcast.21), channel_id=1, source_target_pairs={{0,8},{8,16},{16,24},{24,28},{28,20},{20,12},{12,4},{4,0},{1,9},{9... | collective-permute-start | bytes 1572872 | tf_op jit(solution)/shard_map/ppermute | solution.py:411
  40.7 23.3 %collective-permute-start.27 = (f32[512,256]{1,0:T(8,128)S(1)}, f32[512,256]{1,0:T(8,128)S(1)}, u32[]{:S(2)}, u32[]{:S(2)}) collective-permute-start(f32[512,256]{1,0:T(8,128)S(1)} %bitcast.25), channel_id=1, source_target_pairs={{0,8},{8,16},{16,24},{24,28},{28,20},{20,12},{12,4},{4,0},{1,9},{9... | collective-permute-start | bytes 1572872 | tf_op jit(solution)/shard_map/ppermute | solution.py:411
  49.0 22.5 %collective-permute-start.2 = (f32[512,256]{1,0:T(8,128)S(1)}, f32[512,256]{1,0:T(8,128)S(1)}, u32[]{:S(2)}, u32[]{:S(2)}) collective-permute-start(f32[512,256]{1,0:T(8,128)S(1)} %collective-permute-done.1.refs_4_), channel_id=1, source_target_pairs={{8,0},{16,8},{24,16},{28,24},{20,28},{12,20},{4,12},{0,4},{9,1},{1... | collective-permute-start | bytes 1572872 | tf_op jit(solution)/shard_map/ppermute | solution.py:412
  60.3 22.5 %collective-permute-start.13 = (f32[512,256]{1,0:T(8,128)S(1)}, f32[512,256]{1,0:T(8,128)S(1)}, u32[]{:S(2)}, u32[]{:S(2)}) collective-permute-start(f32[512,256]{1,0:T(8,128)S(1)} %collective-permute-done.12.refs_4_), channel_id=1, source_target_pairs={{8,0},{16,8},{24,16},{28,24},{20,28},{12,20},{4,12},{0,4},{9,1},{1... | collective-permute-start | bytes 1572872 | tf_op jit(solution)/shard_map/ppermute | solution.py:412
  63.0 21.8 %collective-permute-start.23 = (f32[512,256]{1,0:T(8,128)S(1)}, f32[512,256]{1,0:T(8,128)}, u32[]{:S(2)}, u32[]{:S(2)}) collective-permute-start(f32[512,256]{1,0:T(8,128)S(1)} %collective-permute-done.22.refs_1_), channel_id=1, source_target_pairs={{0,8},{8,16},{16,24},{24,28},{28,20},{20,12},{12,4},{4,0},{1,9},{9... | collective-permute-start | bytes 1572872 | tf_op jit(solution)/shard_map/ppermute | solution.py:411
  63.9 25.2 %collective-permute-start.28 = (f32[512,256]{1,0:T(8,128)S(1)}, f32[512,256]{1,0:T(8,128)S(1)}, u32[]{:S(2)}, u32[]{:S(2)}) collective-permute-start(f32[512,256]{1,0:T(8,128)S(1)} %collective-permute-done.27.refs_1_), channel_id=1, source_target_pairs={{0,8},{8,16},{16,24},{24,28},{28,20},{20,12},{12,4},{4,0},{1,9},{9... | collective-permute-start | bytes 1572872 | tf_op jit(solution)/shard_map/ppermute | solution.py:411
  71.5 110.9 %copy-start.16 = (f32[512,256]{1,0:T(8,128)}, f32[512,256]{1,0:T(8,128)S(1)}, u32[]{:S(2)}) copy-start(f32[512,256]{1,0:T(8,128)S(1)} %collective-permute-done.2.refs_6_) | copy-start | bytes 1572868
  71.5 28.9 %collective-permute-start.3 = (f32[512,256]{1,0:T(8,128)S(1)}, f32[512,256]{1,0:T(8,128)S(1)}, u32[]{:S(2)}, u32[]{:S(2)}) collective-permute-start(f32[512,256]{1,0:T(8,128)S(1)} %bitcast.12), channel_id=1, source_target_pairs={{0,8},{8,16},{16,24},{24,28},{28,20},{20,12},{12,4},{4,0},{1,9},{9... | collective-permute-start | bytes 1572872 | tf_op jit(solution)/shard_map/ppermute | solution.py:411
  73.6 27.7 %collective-permute-start.4 = (f32[512,256]{1,0:T(8,128)S(1)}, f32[512,256]{1,0:T(8,128)S(1)}, u32[]{:S(2)}, u32[]{:S(2)}) collective-permute-start(f32[512,256]{1,0:T(8,128)S(1)} %bitcast.13), channel_id=1, source_target_pairs={{8,0},{16,8},{24,16},{28,24},{20,28},{12,20},{4,12},{0,4},{9,1},{1... | collective-permute-start | bytes 1572872 | tf_op jit(solution)/shard_map/ppermute | solution.py:412
  82.7 28.9 %collective-permute-start.14 = (f32[512,256]{1,0:T(8,128)S(1)}, f32[512,256]{1,0:T(8,128)S(1)}, u32[]{:S(2)}, u32[]{:S(2)}) collective-permute-start(f32[512,256]{1,0:T(8,128)S(1)} %bitcast.16), channel_id=1, source_target_pairs={{0,8},{8,16},{16,24},{24,28},{28,20},{20,12},{12,4},{4,0},{1,9},{9... | collective-permute-start | bytes 1572872 | tf_op jit(solution)/shard_map/ppermute | solution.py:411
  84.8 27.7 %collective-permute-start.15 = (f32[512,256]{1,0:T(8,128)S(1)}, f32[512,256]{1,0:T(8,128)S(1)}, u32[]{:S(2)}, u32[]{:S(2)}) collective-permute-start(f32[512,256]{1,0:T(8,128)S(1)} %bitcast.17), channel_id=1, source_target_pairs={{8,0},{16,8},{24,16},{28,24},{20,28},{12,20},{4,12},{0,4},{9,1},{1... | collective-permute-start | bytes 1572872 | tf_op jit(solution)/shard_map/ppermute | solution.py:412
  89.1 33.8 %collective-permute-start.29 = (f32[512,256]{1,0:T(8,128)S(1)}, f32[512,256]{1,0:T(8,128)}, u32[]{:S(2)}, u32[]{:S(2)}) collective-permute-start(f32[512,256]{1,0:T(8,128)S(1)} %collective-permute-done.28.refs_3_), channel_id=1, source_target_pairs={{0,8},{8,16},{16,24},{24,28},{28,20},{20,12},{12,4},{4,0},{1,9},{9... | collective-permute-start | bytes 1572872 | tf_op jit(solution)/shard_map/ppermute | solution.py:411
  100.4 33.8 %collective-permute-start.5 = (f32[512,256]{1,0:T(8,128)S(1)}, f32[512,256]{1,0:T(8,128)}, u32[]{:S(2)}, u32[]{:S(2)}) collective-permute-start(f32[512,256]{1,0:T(8,128)S(1)} %collective-permute-done.3.refs_1_), channel_id=1, source_target_pairs={{0,8},{8,16},{16,24},{24,28},{28,20},{20,12},{12,4},{4,0},{1,9},{9... | collective-permute-start | bytes 1572872 | tf_op jit(solution)/shard_map/ppermute | solution.py:411
  101.3 33.0 %collective-permute-start.6 = (f32[512,256]{1,0:T(8,128)S(1)}, f32[512,256]{1,0:T(8,128)}, u32[]{:S(2)}, u32[]{:S(2)}) collective-permute-start(f32[512,256]{1,0:T(8,128)S(1)} %collective-permute-done.4.refs_2_), channel_id=1, source_target_pairs={{8,0},{16,8},{24,16},{28,24},{20,28},{12,20},{4,12},{0,4},{9,1},{1... | collective-permute-start | bytes 1572872 | tf_op jit(solution)/shard_map/ppermute | solution.py:412
  111.6 33.8 %collective-permute-start.16 = (f32[512,256]{1,0:T(8,128)S(1)}, f32[512,256]{1,0:T(8,128)}, u32[]{:S(2)}, u32[]{:S(2)}) collective-permute-start(f32[512,256]{1,0:T(8,128)S(1)} %collective-permute-done.14.refs_1_), channel_id=1, source_target_pairs={{0,8},{8,16},{16,24},{24,28},{28,20},{20,12},{12,4},{4,0},{1,9},{9... | collective-permute-start | bytes 1572872 | tf_op jit(solution)/shard_map/ppermute | solution.py:411
  112.5 33.0 %collective-permute-start.17 = (f32[512,256]{1,0:T(8,128)S(1)}, f32[512,256]{1,0:T(8,128)}, u32[]{:S(2)}, u32[]{:S(2)}) collective-permute-start(f32[512,256]{1,0:T(8,128)S(1)} %collective-permute-done.15.refs_2_), channel_id=1, source_target_pairs={{8,0},{16,8},{24,16},{28,24},{20,28},{12,20},{4,12},{0,4},{9,1},{1... | collective-permute-start | bytes 1572872 | tf_op jit(solution)/shard_map/ppermute | solution.py:412
  122.9 33.7 %collective-permute-start.24 = (f32[512,256]{1,0:T(8,128)}, f32[512,256]{1,0:T(8,128)}, u32[]{:S(2)}, u32[]{:S(2)}) collective-permute-start(f32[512,256]{1,0:T(8,128)} %collective-permute-done.23.refs_3_), channel_id=1, source_target_pairs={{0,8},{8,16},{16,24},{24,28},{28,20},{20,12},{12,4},{4,0},{1,9},{9... | collective-permute-start | bytes 1572872 | tf_op jit(solution)/shard_map/ppermute | solution.py:411
  134.2 33.7 %collective-permute-start.7 = (f32[512,256]{1,0:T(8,128)}, f32[512,256]{1,0:T(8,128)}, u32[]{:S(2)}, u32[]{:S(2)}) collective-permute-start(f32[512,256]{1,0:T(8,128)} %collective-permute-done.5.refs_3_), channel_id=1, source_target_pairs={{0,8},{8,16},{16,24},{24,28},{28,20},{20,12},{12,4},{4,0},{1,9},{9... | collective-permute-start | bytes 1572872 | tf_op jit(solution)/shard_map/ppermute | solution.py:411
  134.3 40.6 %collective-permute-start.8 = (f32[512,256]{1,0:T(8,128)}, f32[512,256]{1,0:T(8,128)}, u32[]{:S(2)}, u32[]{:S(2)}) collective-permute-start(f32[512,256]{1,0:T(8,128)} %collective-permute-done.6.refs_4_), channel_id=1, source_target_pairs={{8,0},{16,8},{24,16},{28,24},{20,28},{12,20},{4,12},{0,4},{9,1},{1... | collective-permute-start | bytes 1572872 | tf_op jit(solution)/shard_map/ppermute | solution.py:412
  145.4 33.7 %collective-permute-start.18 = (f32[512,256]{1,0:T(8,128)}, f32[512,256]{1,0:T(8,128)}, u32[]{:S(2)}, u32[]{:S(2)}) collective-permute-start(f32[512,256]{1,0:T(8,128)} %collective-permute-done.16.refs_3_), channel_id=1, source_target_pairs={{0,8},{8,16},{16,24},{24,28},{28,20},{20,12},{12,4},{4,0},{1,9},{9... | collective-permute-start | bytes 1572872 | tf_op jit(solution)/shard_map/ppermute | solution.py:411
  145.5 36.9 %collective-permute-start.19 = (f32[512,256]{1,0:T(8,128)}, f32[512,256]{1,0:T(8,128)}, u32[]{:S(2)}, u32[]{:S(2)}) collective-permute-start(f32[512,256]{1,0:T(8,128)} %collective-permute-done.17.refs_4_), channel_id=1, source_target_pairs={{8,0},{16,8},{24,16},{28,24},{20,28},{12,20},{4,12},{0,4},{9,1},{1... | collective-permute-start | bytes 1572872 | tf_op jit(solution)/shard_map/ppermute | solution.py:412
  156.6 36.6 %collective-permute-start.30 = (f32[256,256]{1,0:T(8,128)}, f32[256,256]{1,0:T(8,128)S(1)}, u32[]{:S(2)}, u32[]{:S(2)}) collective-permute-start(f32[256,256]{1,0:T(8,128)} %slice.92), channel_id=1, source_target_pairs={{0,8},{8,16},{16,24},{24,28},{28,20},{20,12},{12,4},{4,0},{1,9},{9... | collective-permute-start | bytes 786440 | tf_op jit(solution)/shard_map/ppermute | solution.py:417
  167.9 27.0 %collective-permute-start.31 = (f32[256,256]{1,0:T(8,128)}, f32[256,256]{1,0:T(8,128)}, u32[]{:S(2)}, u32[]{:S(2)}) collective-permute-start(f32[256,256]{1,0:T(8,128)} %slice.93), channel_id=1, source_target_pairs={{8,0},{16,8},{24,16},{28,24},{20,28},{12,20},{4,12},{0,4},{9,1},{1... | collective-permute-start | bytes 786440 | tf_op jit(solution)/shard_map/ppermute | solution.py:418
  174.9 28.9 %collective-permute-start.25 = (f32[256,256]{1,0:T(8,128)}, f32[256,256]{1,0:T(8,128)}, u32[]{:S(2)}, u32[]{:S(2)}) collective-permute-start(f32[256,256]{1,0:T(8,128)} %slice.90), channel_id=1, source_target_pairs={{0,8},{8,16},{16,24},{24,28},{28,20},{20,12},{12,4},{4,0},{1,9},{9... | collective-permute-start | bytes 786440 | tf_op jit(solution)/shard_map/ppermute | solution.py:417
  179.1 26.5 %collective-permute-start.26 = (f32[256,256]{1,0:T(8,128)}, f32[256,256]{1,0:T(8,128)}, u32[]{:S(2)}, u32[]{:S(2)}) collective-permute-start(f32[256,256]{1,0:T(8,128)} %slice.91), channel_id=1, source_target_pairs={{8,0},{16,8},{24,16},{28,24},{20,28},{12,20},{4,12},{0,4},{9,1},{1... | collective-permute-start | bytes 786440 | tf_op jit(solution)/shard_map/ppermute | solution.py:418
  182.4 43.1 %collective-permute-start.9 = (f32[256,256]{1,0:T(8,128)}, f32[256,256]{1,0:T(8,128)}, u32[]{:S(2)}, u32[]{:S(2)}) collective-permute-start(f32[256,256]{1,0:T(8,128)} %slice.84), channel_id=1, source_target_pairs={{0,8},{8,16},{16,24},{24,28},{28,20},{20,12},{12,4},{4,0},{1,9},{9... | collective-permute-start | bytes 786440 | tf_op jit(solution)/shard_map/ppermute | solution.py:417
  193.2 32.3 %collective-permute-start.10 = (f32[256,256]{1,0:T(8,128)S(1)}, f32[256,256]{1,0:T(8,128)S(1)}, u32[]{:S(2)}, u32[]{:S(2)}) collective-permute-start(f32[256,256]{1,0:T(8,128)S(1)} %copy-done.60), channel_id=1, source_target_pairs={{8,0},{16,8},{24,16},{28,24},{20,28},{12,20},{4,12},{0,4},{9,1},{1... | collective-permute-start | bytes 786440 | tf_op jit(solution)/shard_map/ppermute | solution.py:418
  194.9 20.3 %collective-permute-start.20 = (f32[256,256]{1,0:T(8,128)S(1)}, f32[256,256]{1,0:T(8,128)S(1)}, u32[]{:S(2)}, u32[]{:S(2)}) collective-permute-start(f32[256,256]{1,0:T(8,128)S(1)} %copy-done.61), channel_id=1, source_target_pairs={{0,8},{8,16},{16,24},{24,28},{28,20},{20,12},{12,4},{4,0},{1,9},{9... | collective-permute-start | bytes 786440 | tf_op jit(solution)/shard_map/ppermute | solution.py:417
  195.3 10.3 %copy-start.17 = (f32[512,256]{1,0:T(8,128)S(1)}, f32[512,256]{1,0:T(8,128)}, u32[]{:S(2)}) copy-start(f32[512,256]{1,0:T(8,128)} %copy-done.16) | copy-start | bytes 1572868
  195.4 10.3 %copy-start.20 = (f32[512,256]{1,0:T(8,128)S(1)}, f32[512,256]{1,0:T(8,128)}, u32[]{:S(2)}) copy-start(f32[512,256]{1,0:T(8,128)} %copy-done.19) | copy-start | bytes 1572868
  195.4 10.3 %copy-start.23 = (f32[512,256]{1,0:T(8,128)S(1)}, f32[512,256]{1,0:T(8,128)}, u32[]{:S(2)}) copy-start(f32[512,256]{1,0:T(8,128)} %copy-done.22) | copy-start | bytes 1572868
  195.4 10.3 %copy-start.29 = (f32[512,256]{1,0:T(8,128)S(1)}, f32[512,256]{1,0:T(8,128)}, u32[]{:S(2)}) copy-start(f32[512,256]{1,0:T(8,128)} %copy-done.28) | copy-start | bytes 1572868
  203.8 12.0 %collective-permute-start.21 = (f32[256,256]{1,0:T(8,128)S(1)}, f32[256,256]{1,0:T(8,128)S(1)}, u32[]{:S(2)}, u32[]{:S(2)}) collective-permute-start(f32[256,256]{1,0:T(8,128)S(1)} %copy-done.62), channel_id=1, source_target_pairs={{8,0},{16,8},{24,16},{28,24},{20,28},{12,20},{4,12},{0,4},{9,1},{1... | collective-permute-start | bytes 786440 | tf_op jit(solution)/shard_map/ppermute | solution.py:418
  205.6 10.1 %copy-start.47 = (f32[512,256]{1,0:T(8,128)S(1)}, f32[512,256]{1,0:T(8,128)}, u32[]{:S(2)}) copy-start(f32[512,256]{1,0:T(8,128)} %copy-done.46) | copy-start | bytes 1572868
  205.6 10.1 %copy-start.50 = (f32[512,256]{1,0:T(8,128)S(1)}, f32[512,256]{1,0:T(8,128)}, u32[]{:S(2)}) copy-start(f32[512,256]{1,0:T(8,128)} %copy-done.49) | copy-start | bytes 1572868
  205.6 48.5 %collective-permute-start.32 = (f32[256,1024]{1,0:T(8,128)}, f32[256,1024]{1,0:T(8,128)}, u32[]{:S(2)}, u32[]{:S(2)}) collective-permute-start(f32[256,1024]{1,0:T(8,128)} %get-tuple-element.22), channel_id=1, source_target_pairs={{0,1},{1,0},{2,3},{3,2},{4,5},{5,4},{6,7},{7,6},{8,9},{9,8},{10,11... | collective-permute-start | bytes 3145736 | tf_op jit(solution)/shard_map/ppermute | solution.py:431
  215.2 9.3 %copy-start.54 = (f32[256,256]{1,0:T(8,128)}, f32[256,256]{1,0:T(8,128)S(1)}, u32[]{:S(2)}) copy-start(f32[256,256]{1,0:T(8,128)S(1)} %collective-permute-done.20.refs_7_) | copy-start | bytes 786436
  215.2 10.4 %copy-start.38 = (f32[512,256]{1,0:T(8,128)S(1)}, f32[512,256]{1,0:T(8,128)}, u32[]{:S(2)}) copy-start(f32[512,256]{1,0:T(8,128)} %copy-done.37) | copy-start | bytes 1572868
  215.2 10.4 %copy-start.41 = (f32[512,256]{1,0:T(8,128)S(1)}, f32[512,256]{1,0:T(8,128)}, u32[]{:S(2)}) copy-start(f32[512,256]{1,0:T(8,128)} %copy-done.40) | copy-start | bytes 1572868
  215.2 41.7 %collective-permute-start.34 = (f32[256,1024]{1,0:T(8,128)}, f32[256,1024]{1,0:T(8,128)}, u32[]{:S(2)}, u32[]{:S(2)}) collective-permute-start(f32[256,1024]{1,0:T(8,128)} %get-tuple-element.24), channel_id=1, source_target_pairs={{0,1},{1,0},{2,3},{3,2},{4,5},{5,4},{6,7},{7,6},{8,9},{9,8},{10,11... | collective-permute-start | bytes 3145736 | tf_op jit(solution)/shard_map/ppermute | solution.py:431
  215.7 8.8 %copy-start.56 = (f32[256,256]{1,0:T(8,128)}, f32[256,256]{1,0:T(8,128)S(1)}, u32[]{:S(2)}) copy-start(f32[256,256]{1,0:T(8,128)S(1)} %collective-permute-done.21.refs_8_) | copy-start | bytes 786436
  225.5 10.3 %copy-start.58 = (f32[128]{0:T(128)S(1)}, f32[128]{0:T(128)}, u32[]{:S(2)}) copy-start(f32[128]{0:T(128)} %virt_ref.1) | copy-start | bytes 1540
  225.5 10.3 %copy-start.65 = (f32[32]{0:T(128)S(1)}, f32[32]{0:T(128)}, u32[]{:S(2)}) copy-start(f32[32]{0:T(128)} %param.16) | copy-start | bytes 388
  225.5 10.7 %copy-start.63 = (s32[16,16]{1,0:T(8,128)S(1)}, s32[16,16]{1,0:T(8,128)}, u32[]{:S(2)}) copy-start(s32[16,16]{1,0:T(8,128)} %param.12) | copy-start | bytes 3076
  225.5 33.3 %collective-permute-start.36 = (f32[256,1024]{1,0:T(8,128)}, f32[256,1024]{1,0:T(8,128)}, u32[]{:S(2)}, u32[]{:S(2)}) collective-permute-start(f32[256,1024]{1,0:T(8,128)} %get-tuple-element.26), channel_id=1, source_target_pairs={{0,1},{1,0},{2,3},{3,2},{4,5},{5,4},{6,7},{7,6},{8,9},{9,8},{10,11... | collective-permute-start | bytes 3145736 | tf_op jit(solution)/shard_map/ppermute | solution.py:431
  225.5 8.8 %copy-start.52 = (f32[256,256]{1,0:T(8,128)}, f32[256,256]{1,0:T(8,128)S(1)}, u32[]{:S(2)}) copy-start(f32[256,256]{1,0:T(8,128)S(1)} %collective-permute-done.10.refs_8_) | copy-start | bytes 786436
  235.3 26.2 %collective-permute-start.38 = (f32[256,1024]{1,0:T(8,128)}, f32[256,1024]{1,0:T(8,128)}, u32[]{:S(2)}, u32[]{:S(2)}) collective-permute-start(f32[256,1024]{1,0:T(8,128)} %get-tuple-element.28), channel_id=1, source_target_pairs={{0,1},{1,0},{2,3},{3,2},{4,5},{5,4},{6,7},{7,6},{8,9},{9,8},{10,11... | collective-permute-start | bytes 3145736 | tf_op jit(solution)/shard_map/ppermute | solution.py:431
  236.3 20.6 %copy-start.4 = (f32[256,1024]{1,0:T(8,128)S(1)}, f32[256,1024]{1,0:T(8,128)}, u32[]{:S(2)}) copy-start(f32[256,1024]{1,0:T(8,128)} %copy-done.3) | copy-start | bytes 3145732
  255.3 40.1 %collective-permute-start.33 = (f32[128,1024]{1,0:T(8,128)S(1)}, f32[128,1024]{1,0:T(8,128)S(1)}, u32[]{:S(2)}, u32[]{:S(2)}) collective-permute-start(f32[128,1024]{1,0:T(8,128)S(1)} %slice_add_fusion.3), channel_id=1, source_target_pairs={{0,2},{1,3},{2,0},{3,1},{4,6},{5,7},{6,4},{7,5},{8,10},{9,11},{10,... | collective-permute-start | bytes 1572872 | tf_op jit(solution)/shard_map/ppermute | solution.py:433
  258.2 37.2 %collective-permute-start.35 = (f32[128,1024]{1,0:T(8,128)S(1)}, f32[128,1024]{1,0:T(8,128)S(1)}, u32[]{:S(2)}, u32[]{:S(2)}) collective-permute-start(f32[128,1024]{1,0:T(8,128)S(1)} %slice_add_fusion.2), channel_id=1, source_target_pairs={{0,2},{1,3},{2,0},{3,1},{4,6},{5,7},{6,4},{7,5},{8,10},{9,11},{10,... | collective-permute-start | bytes 1572872 | tf_op jit(solution)/shard_map/ppermute | solution.py:433
  259.9 35.5 %collective-permute-start.37 = (f32[128,1024]{1,0:T(8,128)S(1)}, f32[128,1024]{1,0:T(8,128)S(1)}, u32[]{:S(2)}, u32[]{:S(2)}) collective-permute-start(f32[128,1024]{1,0:T(8,128)S(1)} %slice_add_fusion.1), channel_id=1, source_target_pairs={{0,2},{1,3},{2,0},{3,1},{4,6},{5,7},{6,4},{7,5},{8,10},{9,11},{10,... | collective-permute-start | bytes 1572872 | tf_op jit(solution)/shard_map/ppermute | solution.py:433
  262.7 40.3 %collective-permute-start.39 = (f32[128,1024]{1,0:T(8,128)S(1)}, f32[128,1024]{1,0:T(8,128)S(1)}, u32[]{:S(2)}, u32[]{:S(2)}) collective-permute-start(f32[128,1024]{1,0:T(8,128)S(1)} %slice_add_fusion), channel_id=1, source_target_pairs={{0,2},{1,3},{2,0},{3,1},{4,6},{5,7},{6,4},{7,5},{8,10},{9,11},{10,... | collective-permute-start | bytes 1572872 | tf_op jit(solution)/shard_map/ppermute | solution.py:433
  (45 other events, 228.5 us)
Sparse Core Ops, SparseCore 0:
  9.0 37.1 all-gather.4

commit v2 on v1

v2 whole, which is shorter than its diff:
```python
import functools

import jax
import jax.numpy as jnp
from jax import lax
from jax.experimental import pallas as pl
from jax.experimental.pallas import tpu as pltpu
from jax.sharding import PartitionSpec as P

LANES = 128
PARTS = 4
VMEM_MIB = 64


def cost(flops, moved):
    return pl.CostEstimate(flops=flops // 1000, bytes_accessed=moved // 1000, transcendentals=0)

F32 = jnp.float32
BF16 = jnp.bfloat16
HBM = pl.BlockSpec(memory_space=pltpu.HBM)
VMEM = pl.BlockSpec(memory_space=pltpu.VMEM)
SMEM = pl.BlockSpec(memory_space=pltpu.SMEM)


def params(mib):
    return pltpu.CompilerParams(vmem_limit_bytes=mib << 20)


def split(x):
    high = x.astype(BF16)
    return high, (x - high.astype(F32)).astype(BF16)


def dot(x, y):
    return jnp.dot(x, y, preferred_element_type=F32)


def swap_groups(arrays, group):
    arrays = list(arrays)
    count = len(arrays)
    lane = lax.broadcasted_iota(jnp.int32, arrays[0].shape, 1) // group
    bit = 1
    while bit < count:
        odd = (lane & bit) != 0
        for low in range(count):
            if low & bit:
                continue
            high = low | bit
            up = pltpu.roll(arrays[high], bit * group, 1)
            down = pltpu.roll(arrays[low], LANES - bit * group, 1)
            arrays[low], arrays[high] = (
                jnp.where(odd, up, arrays[low]),
                jnp.where(odd, arrays[high], down),
            )
        bit *= 2
    return arrays


def ladder_prep_kernel(blocks_ref, *refs):
    out_ref = refs[-1]
    slots, virt, _ = blocks_ref.shape[1:]
    parts = out_ref.shape[0]
    part = virt // parts
    per = LANES // part
    for first in range(0, slots, per):
        pieces = [blocks_ref[0, first + s] for s in range(per)]
        for q, piece in enumerate(swap_groups(pieces, part)):
            high, low = split(piece)
            lanes = pl.ds(first * part, LANES)
            out_ref[q, 0, 0:virt, lanes] = high
            out_ref[q, 0, virt : 2 * virt, lanes] = low


def ladder_prep(blocks, parts, first, count, before):
    a_here, slots, virt, _ = blocks.shape
    depth = slots * (virt // parts)
    again = before is not None
    spare = -(-(VMEM_MIB << 20) // (parts * a_here * 2 * virt * depth * 2))
    return pl.pallas_call(
        ladder_prep_kernel,
        grid=(count,),
        in_specs=[pl.BlockSpec((1, slots, virt, virt), lambda a: (first + a, 0, 0, 0))] + [HBM] * again,
        out_specs=pl.BlockSpec((parts, 1, 2 * virt, depth), lambda a: (0, first + a, 0, 0)),
        out_shape=jax.ShapeDtypeStruct(((1 + spare) * parts, a_here, 2 * virt, depth), BF16),
        input_output_aliases={1: 0} if again else {},
        compiler_params=params(12),
        cost_estimate=cost(8 * blocks.size * count // a_here, 8 * blocks.size * count // a_here),
        name="ladder_prep",
    )(blocks, *([before] if again else []))


def mirrored(rel, size):
    out = 0
    bit = 1
    while bit < size:
        out = out * 2 + (rel // bit) % 2
        bit *= 2
    return out


def cycle_prep_kernel(place_ref, index_ref, blocks_ref, high_ref, low_ref, dense):
    shares, occ, slots, a_here, virt = blocks_ref.shape
    i_here = occ // shares
    mine = place_ref[0]
    dense[...] = jnp.zeros_like(dense)
    for owner in range(shares):
        rel = mine ^ owner
        base = mirrored(rel, shares) * i_here

        @pl.loop(0, i_here)
        def _(i):
            for share in range(shares):
                for s in range(slots):
                    row = (share * occ + owner * i_here + i) * slots + s
                    k = index_ref[row] - mine * i_here

                    @pl.when((k >= 0) & (k < i_here))
                    def _():
                        lanes = pl.ds(pl.multiple_of(k * virt, virt), virt)
                        dense[base + i, :, lanes] = blocks_ref[share, owner * i_here + i, s]

    rows = occ * a_here
    step = i_here * a_here
    for first in range(shares):
        piece = dense[first * i_here : (first + 1) * i_here].reshape(step, i_here * virt)
        high, low = split(piece)
        high_ref[first * step : (first + 1) * step, :] = high
        low_ref[first * step : (first + 1) * step, :] = low


def cycle_prep(place, index, blocks):
    shares, occ, slots, a_here, virt = blocks.shape
    shape = jax.ShapeDtypeStruct((occ * a_here, occ // shares * virt), BF16)
    return pl.pallas_call(
        cycle_prep_kernel,
        in_specs=[SMEM, SMEM, VMEM],
        out_specs=[VMEM, VMEM],
        out_shape=[shape, shape],
        scratch_shapes=[pltpu.VMEM((occ, a_here, occ // shares * virt), F32)],
        compiler_params=params(12),
        cost_estimate=cost(2 * blocks.size, 8 * blocks.size),
        name="cycle_prep",
    )(place, index, blocks)


def place_blocks(layout, source_ref, block_refs, store):
    rows_each = layout[0][2]
    for (owner, offset, rows), block in zip(layout, block_refs):
        store(pl.multiple_of(source_ref[owner] * rows_each + offset, rows), rows, block)


def cycle_kernel(layout, part, occ, source_ref, *refs):
    count = len(layout)
    high_ref, low_ref, keep_ref, send_ref, held, cols_high, cols_low = refs[count:]
    halves, rows, _ = held.shape
    virt = rows // part

    def store(start, rows, block):
        @pl.loop(0, rows // part)
        def _(c):
            here = pl.ds(pl.multiple_of(c * part, part), part)
            there = pl.ds(pl.multiple_of(start + c * part, part), part)
            for h in range(halves):
                held[h, there, :] = block[here, h * LANES : (h + 1) * LANES]

    place_blocks(layout, source_ref, refs[:count], store)
    per = LANES // occ
    half_rows = keep_ref.shape[0]
    width = 2 * LANES
    steps = part // per

    for first in range(0, steps, 2):
        for g in range(first, first + 2):
            for h in range(halves):
                pieces = [held[h, pl.ds(g * per + m, virt, stride=part), :] for m in range(per)]
                for m, piece in enumerate(swap_groups(pieces, occ)):
                    k = h * per + m
                    high, low = split(piece)
                    lanes = pl.ds(g * LANES, LANES)
                    cols_high[k * virt : (k + 1) * virt, lanes] = high
                    cols_low[k * virt : (k + 1) * virt, lanes] = low
        lanes = pl.ds(first * LANES, width)
        right_high = cols_high[:, lanes]
        right_low = cols_low[:, lanes]
        for out_ref, top in ((send_ref, half_rows), (keep_ref, 0)):
            left_high = high_ref[top : top + half_rows, :]
            left_low = low_ref[top : top + half_rows, :]
            out_ref[:, lanes] = (
                dot(left_high, right_high) + dot(left_low, right_high) + dot(left_high, right_low)
            )


def cycle_part(layout, part, virt, occ, source, blocks, high, low):
    cols = blocks[0].shape[1]
    halves = cols // LANES
    rows, depth = high.shape
    wide = part * occ
    shape = jax.ShapeDtypeStruct((rows // 2, wide), F32)
    return pl.pallas_call(
        functools.partial(cycle_kernel, layout, part, occ),
        in_specs=[SMEM] + [VMEM] * len(blocks) + [VMEM, VMEM],
        out_specs=[VMEM, VMEM],
        out_shape=[shape, shape],
        scratch_shapes=[
            pltpu.VMEM((halves, virt * part, LANES), F32),
            pltpu.VMEM((depth, wide), BF16),
            pltpu.VMEM((depth, wide), BF16),
        ],
        compiler_params=params(18),
        cost_estimate=cost(6 * rows * depth * wide, 4 * virt * part * cols),
        name="cycle_part",
    )(source, *blocks, high, low)


def ladder_kernel(layout, part, q, again, last, source_ref, index_ref, *refs):
    count = len(layout)
    left_hbm = refs[count]
    before_ref = refs[count + 1] if again else None
    energies = refs[count + 1 + again : count + 1 + again + 3 * last]
    out_ref, left, held_high, held_low, right_high, right_low, sem = refs[
        count + 1 + again + 3 * last :
    ]
    a_here, virt, _ = out_ref.shape
    slots = right_high.shape[0] // part
    groups = sem.shape[0]
    each = a_here // groups
    copies = [
        pltpu.make_async_copy(
            left_hbm.at[q, pl.ds(n * each, each)], left.at[pl.ds(n * each, each)], sem.at[n]
        )
        for n in range(groups)
    ]
    for copy in copies:
        copy.start()

    def store(start, rows, block):
        @pl.loop(0, rows // part)
        def _(c):
            there = pl.ds(pl.multiple_of(start + c * part, part), part)
            high, low = split(block[pl.ds(pl.multiple_of(c * part, part), part), :])
            held_high[there, :] = high
            held_low[there, :] = low

    place_blocks(layout, source_ref, refs[:count], store)

    for n in range(groups):
        copies[n].wait()

        @pl.loop(n * each, (n + 1) * each)
        def _(a):
            for s in range(slots):
                rows = pl.ds(pl.multiple_of(index_ref[a * slots + s] * part, part), part)
                right_high[s * part : (s + 1) * part, :] = held_high[rows, :]
                right_low[s * part : (s + 1) * part, :] = held_low[rows, :]
            both = dot(left[a], right_high[...])
            total = both[:virt] + both[virt:] + dot(left[a, :virt], right_low[...])
            if again:
                total = total + before_ref[a]
            if last:
                energy_a, energy_b, energy_ij = energies
                low = (energy_a[pl.ds(a, 1), :] + energy_b[...]) - energy_ij[...]
                row = lax.broadcasted_iota(jnp.int32, total.shape, 0)
                total = jnp.where(row < virt - part, total / low, total)
            out_ref[a] = total


def ladder_part(layout, part, q, source, index, blocks, left, before, energies):
    cols = blocks[0].shape[1]
    _, a_here, rows, depth = left.shape
    virt = rows // 2
    again = before is not None
    last = len(energies) > 0
    return pl.pallas_call(
        functools.partial(ladder_kernel, layout, part, q, again, last),
        in_specs=[SMEM, SMEM] + [VMEM] * len(blocks) + [HBM] + [VMEM] * (again + len(energies)),
        out_specs=VMEM,
        out_shape=jax.ShapeDtypeStruct((a_here, virt, cols), F32),
        scratch_shapes=[
            pltpu.VMEM((a_here, rows, depth), BF16),
            pltpu.VMEM((virt * part, cols), BF16),
            pltpu.VMEM((virt * part, cols), BF16),
            pltpu.VMEM((depth, cols), BF16),
            pltpu.VMEM((depth, cols), BF16),
            pltpu.SemaphoreType.DMA((4,)),
        ],
        input_output_aliases={3 + len(blocks): 0} if again else {},
        compiler_params=params(18),
        cost_estimate=cost(3 * a_here * rows * depth * cols, 2 * left.size // left.shape[0]),
        name="ladder_part",
    )(source, index, *blocks, left, *([before] if again else []), *energies)


def join_kernel(q, part, occ, last, *refs):
    energy_a, energy_b, energy_ij, keep_ref, near_ref, far_ref, total_ref, out_ref, held = refs
    a_here, virt, cols = total_ref.shape
    halves = cols // LANES
    per = LANES // occ

    @pl.loop(0, part // per)
    def _(g):
        lanes = pl.ds(pl.multiple_of(g * LANES, LANES), LANES)
        for h in range(halves):
            pieces = []
            for m in range(per):
                here = pl.ds((h * per + m) * a_here, a_here)
                pieces.append(keep_ref[here, lanes] + near_ref[here, lanes] + far_ref[here, lanes])
            for m, piece in enumerate(swap_groups(pieces, occ)):
                held[h, pl.ds(g * per + m, a_here, stride=part), :] = piece

    @pl.loop(0, a_here)
    def _(a):
        for first in range(0, virt, part):
            rows = slice(first, first + part)
            total = total_ref[a, rows, :]
            if first == q * part:
                here = pl.ds(pl.multiple_of(a * part, part), part)
                total = total + jnp.concatenate([held[h, here, :] for h in range(halves)], axis=1)
                if last:
                    low = (energy_a[pl.ds(a, 1), :] + energy_b[rows, :]) - energy_ij[...]
                    total = total / low
            out_ref[a, rows, :] = total


def join(q, part, occ, last, energies, keep, near, far, total):
    a_here, _, cols = total.shape
    return pl.pallas_call(
        functools.partial(join_kernel, q, part, occ, last),
        in_specs=[VMEM] * (len(energies) + 4),
        out_specs=VMEM,
        out_shape=jax.ShapeDtypeStruct(total.shape, F32),
        scratch_shapes=[pltpu.VMEM((cols // LANES, a_here * part, LANES), F32)],
        input_output_aliases={len(energies) + 3: 0},
        compiler_params=params(18),
        cost_estimate=cost(8 * a_here * part * cols, 20 * a_here * part * cols),
        name="join",
    )(*energies, keep, near, far, total)


def ring_order(size):
    return list(range(0, size, 2)) + list(range(size - 1 - size % 2, 0, -2))


def per_device(
    amplitudes, ladder_blocks, ladder_index, cycle_blocks, cycle_index, eps_virt, eps_occ
):
    virt = eps_virt.shape[0]
    occ = eps_occ.shape[0]
    rows_here, cols = amplitudes.shape
    a_here = rows_here // virt
    i_here = cols // occ
    wide = lax.axis_size("wide")
    narrow = lax.axis_size("narrow")
    wide_pos = lax.axis_index("wide")
    narrow_pos = lax.axis_index("narrow")
    parts = PARTS
    part = virt // parts

    order = ring_order(wide)
    ahead = [(order[r], order[(r + 1) % wide]) for r in range(wide)]
    back = [(order[(r + 1) % wide], order[r]) for r in range(wide)]
    order_now = jnp.asarray(order, jnp.int32)
    spot = jnp.asarray([order.index(w) for w in range(wide)], jnp.int32)[wide_pos]
    steps = (wide - 1) // 2
    shifts = [0]
    for s in range(1, steps + 1):
        shifts += [-s, s]
    if wide % 2 == 0:
        shifts.append(wide // 2)
    source = order_now[(spot + jnp.asarray(shifts, jnp.int32)) % wide]

    own = amplitudes.reshape(a_here, virt, cols)
    rows_each = a_here * part

    hops = steps + (wide % 2 == 0)
    meet = hops // 2
    half = rows_each // 2
    layout = [(0, 0, rows_each)]
    for s in range(steps):
        layout += [(2 * s + 1, 0, rows_each), (2 * s + 2, 0, rows_each)]
    if wide % 2 == 0:
        layout += [(wide - 1, 0, half), (wide - 1, half, rows_each - half)]

    def tie(x, *others):
        return lax.optimization_barrier((x, *others))[0]

    ring = []
    for q in range(parts):
        whole = tie(own, ring[0][1]) if q else own
        block = whole[:, q * part : (q + 1) * part, :].reshape(rows_each, cols)
        ring.append([[block], block, block])

    token = []

    def ordered(x):
        return tie(x, *token) if token else x

    def hop(q, s, wait):
        blocks, right, left = ring[q]
        if wait:
            right, left, *_ = lax.optimization_barrier((right, left, *wait))
        if s == steps:
            right, left = right[:half], left[half:]
        right = lax.ppermute(right, "wide", ahead)
        left = lax.ppermute(left, "wide", back)
        blocks += [right, left]
        ring[q][1:] = [right, left]

    energy_a = lax.dynamic_slice_in_dim(eps_virt, wide_pos * a_here, a_here, 0)
    energy_i = lax.dynamic_slice_in_dim(eps_occ, narrow_pos * i_here, i_here, 0)
    energy_ij = (energy_i[:, None] + eps_occ[None, :]).reshape(1, cols)
    energies = [
        jnp.broadcast_to(energy_a[:, None], (a_here, cols)),
        jnp.broadcast_to(eps_virt[:, None], (virt, cols)),
        energy_ij,
    ]

    ladder_list = ladder_index.reshape(-1)
    keeps, nears, passes, fars = ([None] * parts for _ in range(4))
    total = None

    def cycle(q):
        blocks = [ordered(ring[q][0][0])] + ring[q][0][1:]
        keeps[q], send = cycle_part(layout, part, virt, occ, source, blocks, *dense)
        nears[q] = lax.ppermute(send, "narrow", [(n, n ^ 1) for n in range(narrow)])
        token[:] = [keeps[q]]

    def pass_on(q):
        keep = ordered(keeps[q])
        rows = keep.shape[0]
        passes[q] = keep[rows // 2 :] + nears[q][rows // 2 :]
        token[:] = [passes[q]]
        fars[q] = lax.ppermute(passes[q], "narrow", [(n, n ^ 2) for n in range(narrow)])

    def ladder(q, total):
        blocks = [ordered(ring[q][0][0])] + ring[q][0][1:]
        final = energies if q == parts - 1 else []
        total = ladder_part(
            layout, part, q, source, ladder_list, blocks, split_left, total, final
        )
        token[:] = [total]
        return total

    def add(q, total):
        last = q == parts - 1
        total = join(
            q, part, occ, last, energies, keeps[q], nears[q], fars[q], ordered(total)
        )
        token[:] = [total]
        return total

    def prepare(n, before):
        pieces = 4
        each = a_here // pieces
        out = ladder_prep(ordered(ladder_blocks), parts, n * each, each, before)
        token[:] = [out]
        return out

    walk = [[(0, s)] for s in range(meet)]
    for q in range(parts):
        rest = [(q, s) for s in range(meet, hops)]
        following = [(q + 1, s) for s in range(meet)] if q + 1 < parts else []
        for n in range(max(len(rest), len(following))):
            walk.append(rest[n : n + 1] + following[n : n + 1])
    whole_at = [max(n for n, step in enumerate(walk) if (q, hops - 1) in step) for q in range(parts)]

    last = parts - 1
    split_left = total = dense = None
    index_all = cycle_all = None
    place = narrow_pos.reshape(1).astype(jnp.int32)
    prepared = 0
    due = []
    for n, step in enumerate(walk):
        for q, s in step:
            hop(q, s, due)
        due = []
        if n == 0:
            index_all = lax.all_gather(cycle_index, "narrow", axis=0).reshape(-1)
            picked = lax.dynamic_slice_in_dim(
                tie(cycle_blocks, ring[0][0][0]), wide_pos * a_here, a_here, 2
            )
            cycle_all = lax.all_gather(picked, "narrow", axis=0)
        if prepared < 4:
            for _ in step:
                split_left = prepare(prepared, split_left)
                prepared += 1
        elif dense is None:
            dense = cycle_prep(place, ordered(index_all), cycle_all)
            token[:] = [dense[0]]
        for q in range(last):
            if n == whole_at[q] + 1:
                cycle(q)
            if n == whole_at[q] + 2:
                if q < last - 1:
                    total = ladder(q, total)
                pass_on(q)
            if n == whole_at[q] + 3:
                due.append(fars[q])
        due += token
    total = ladder(last - 1, total)
    cycle(last)
    for q in range(last - 1):
        total = add(q, total)
    token.append(fars[last - 1])
    pass_on(last)
    total = add(last - 1, total)
    total = ladder(last, total)
    total = add(last, total)
    return total.reshape(rows_here, cols)


def solution(mesh):
    in_specs = (
        P("wide", "narrow"),
        P("wide", None, None, None),
        P("wide", None),
        P(None, "narrow", None, None),
        P(None, "narrow"),
        P(),
        P(),
    )
    out_specs = P("wide", "narrow")
    return jax.shard_map(
        per_device, mesh=mesh, in_specs=in_specs, out_specs=out_specs, check_vma=False
    )
```

time: 323 us -> 267 us (0.83)
  waiting for transfers between devices: 120 us -> 55.7 us
  Pallas kernels: 99.3 us -> 110 us
    ppermute x40, waiting for transfers between devices: 120 us -> 55.7 us  [the longest x16 23.9 us: hop(): right = lax.ppermute(right, 'wide', ahead)]
    pallas_call x6 -> x12, Pallas kernels: 58.5 us -> 72 us  [the longest x4 35.7 us: ladder_part(): pl.pallas_call(functools.partial(ladder_kernel, layout, part, q, again, l...]
    unnamed x136, local copies, waits for them, and re-layouts: 17 us -> 27 us
    slice x9 -> x10, local copies, waits for them, and re-layouts: 13.2 us -> 5.57 us  [the longest x8 3.57 us: hop(): right, left = (right[:half], left[half:])]
  transfers between devices with their start and end apart: 41 -> 41, of which waited for: 16 -> 17; matrix products, arithmetic and copies ran while one was open for 6% -> 4% of each run, Pallas kernels for 28% -> 37%
where the time goes in v2:
time: 267 us; the launch traced here: 266 us
  Pallas kernels  110 us (41%)
  waiting for transfers between devices  55.7 us (21%)
  starting transfers between devices  40.4 us (15%)
  local copies, waits for them, and re-layouts  37.1 us (14%)
  between operations  14.1 us (5%)
  blocking collectives  5.15 us (2%)
  other arithmetic  2.98 us (1%)
    pallas_call x4, Pallas kernels, ladder_part(): pl.pallas_call(functools.partial(ladder_kernel, layout, part, q, again, l...  35.7 us
    pallas_call x4, Pallas kernels, cycle_part(): pl.pallas_call(functools.partial(cycle_kernel, layout, part, occ), in_spe...  31.9 us
    unnamed x136, local copies, waits for them, and re-layouts  27 us
    ppermute x16, starting transfers between devices, hop(): right = lax.ppermute(right, 'wide', ahead)  25.5 us
    ppermute x16, waiting for transfers between devices, hop(): right = lax.ppermute(right, 'wide', ahead)  23.9 us
    ppermute x16, waiting for transfers between devices, hop(): left = lax.ppermute(left, 'wide', back)  21.1 us
    pallas_call x4, Pallas kernels, join(): pl.pallas_call(functools.partial(join_kernel, q, part, occ, last), in_spe...  19.4 us
    pallas_call x4, Pallas kernels, ladder_prep(): pl.pallas_call(ladder_prep_kernel, grid=(count,), in_specs=[pl.BlockSpec(...  16.8 us
  transfers between devices with their start and end apart: 41, of which 17 were waited for; matrix products, arithmetic and copies ran while one was open for 4% of the time, Pallas kernels for 37%

profile of v2, /device:TPU:0, one launch (start us, length us, event | category | flops | bytes accessed | tf_op | source)
XLA Modules:
  0.0 265.7 jit_solution(10497492052401416134)
XLA Ops:
  6.5 1.1 slice.82
  7.6 2.5 constant_dynamic-slice_fusion
  10.2 3.1 %collective-permute-start = (f32[512,256]{1,0:T(8,128)S(1)}, f32[512,256]{1,0:T(8,128)S(1)}, u32[]{:S(2)}, u32[]{:S(2)}) collective-permute-start(f32[512,256]{1,0:T(8,128)S(1)} %bitcast.10), channel_id=1, source_target_pairs={{0,8},{8,16},{16,24},{24,28},{28,20},{20,12},{12,4},{4,0},{1,9},{9... | collective-permute-start | bytes 1572872 | tf_op jit(solution)/shard_map/ppermute | solution.py:403
  13.3 5.8 %copy-done = f32[16,16,128,128]{3,2,1,0:T(8,128)S(1)} copy-done((f32[16,16,128,128]{3,2,1,0:T(8,128)S(1)}, f32[16,16,128,128]{3,2,1,0:T(8,128)}, u32[]{:S(2)}) %copy-start) | copy-done | bytes 16777240
  19.1 4.2 %ladder_prep.4.refs_0_ = bf16[20,16,256,512]{3,2,1,0:T(8,128)(2,1)} custom-call(f32[16,16,128,128]{3,2,1,0:T(8,128)S(1)} %copy-done), custom_call_target="tpu_custom_call" | custom-call | flops 8388 | bytes 8388 | tf_op jit(solution)/shard_map/ladder_prep/pallas_call | solution.py:79
  23.3 1.8 collective-permute-done.refs_1_
  25.1 1.5 collective-permute-done.1.refs_2_
  26.6 1.6 collective-permute-start.2
  28.7 4.2 %ladder_prep.5.refs_0_ = bf16[20,16,256,512]{3,2,1,0:T(8,128)(2,1)} custom-call(f32[16,16,128,128]{3,2,1,0:T(8,128)S(1)} %copy-done, bf16[20,16,256,512]{3,2,1,0:T(8,128)(2,1)} %ladder_prep.4.refs_0_), custom_call_target="tpu_custom_call", output_to_operand_aliasing={{}: (1, {})} | custom-call | flops 8388 | bytes 8388 | tf_op jit(solution)/shard_map/ladder_prep/pallas_call | solution.py:79
  32.9 6.4 %collective-permute-done.2.refs_3_ = f32[512,256]{1,0:T(8,128)S(1)} collective-permute-done((f32[512,256]{1,0:T(8,128)S(1)}, f32[512,256]{1,0:T(8,128)S(1)}, u32[]{:S(2)}, u32[]{:S(2)}) %collective-permute-start.2) | collective-permute-done | bytes 524320 | tf_op jit(solution)/shard_map/ppermute | solution.py:403
  39.2 1.3 collective-permute-done.3.refs_4_
  40.5 1.6 collective-permute-start.4
  43.5 1.6 collective-permute-start.9
  45.5 5.2 %all-gather.2 = s32[4,32,4]{1,2,0:T(4,128)S(1)} all-gather(s32[1,32,4]{1,2,0:T(4,128)S(1)} %bitcast.29), channel_id=2, replica_groups=mesh['wide'=8,'narrow'=4] {'narrow'}, dimensions={0}, use_global_device_ids=true | all-gather | bytes 2560 | tf_op jit(solution)/shard_map/all_gather | solution.py:477
  51.5 5.8 %copy-done.1 = f32[16,16,128,128]{3,2,1,0:T(8,128)S(1)} copy-done((f32[16,16,128,128]{3,2,1,0:T(8,128)S(1)}, f32[16,16,128,128]{3,2,1,0:T(8,128)}, u32[]{:S(2)}) %copy-start.1) | copy-done | bytes 16777240
  57.3 4.2 %ladder_prep.6.refs_0_ = bf16[20,16,256,512]{3,2,1,0:T(8,128)(2,1)} custom-call(f32[16,16,128,128]{3,2,1,0:T(8,128)S(1)} %copy-done.1, bf16[20,16,256,512]{3,2,1,0:T(8,128)(2,1)} %ladder_prep.5.refs_0_), custom_call_target="tpu_custom_call", output_to_operand_aliasing={{}: (1, {})} | custom-call | flops 8388 | bytes 8388 | tf_op jit(solution)/shard_map/ladder_prep/pallas_call | solution.py:79
  61.6 4.2 %ladder_prep.7.refs_9_ = bf16[20,16,256,512]{3,2,1,0:T(8,128)(2,1)} custom-call(f32[16,16,128,128]{3,2,1,0:T(8,128)S(1)} %copy-done.1, bf16[20,16,256,512]{3,2,1,0:T(8,128)(2,1)} %ladder_prep.6.refs_0_), custom_call_target="tpu_custom_call", output_to_operand_aliasing={{}: (1, {})} | custom-call | flops 8388 | bytes 8388 | tf_op jit(solution)/shard_map/ladder_prep/pallas_call | solution.py:79
  66.6 1.6 collective-permute-start.6
  70.7 1.6 collective-permute-start.11
  72.8 2.2 copy-done.8
  75.1 6.4 %cycle_prep.1 = (bf16[512,1024]{1,0:T(8,128)(2,1)S(1)}, bf16[512,1024]{1,0:T(8,128)(2,1)S(1)}) custom-call(s32[1]{0:T(128)} %bitcast.6.place_ref, s32[512]{0:T(512)S(1)} %reshape.61.index_ref, f32[4,32,4,16,128]{4,3,2,1,0:T(8,128)S(1)} %bitcast.26), custom_call_target="tpu_custom_call" | custom-call | flops 2097 | bytes 8388 | tf_op jit(solution)/shard_map/cycle_prep/pallas_call | solution.py:134
  81.6 8.2 %cycle_part.4 = (f32[256,1024]{1,0:T(8,128)S(1)}, f32[256,1024]{1,0:T(8,128)}) custom-call(s32[8]{0:T(128)S(1)} %gather_fusion, f32[512,256]{1,0:T(8,128)S(1)} %bitcast.12, f32[512,256]{1,0:T(8,128)S(1)} %copy-done.37, f32[512,256]{1,0:T(8,128)S(1)} %copy-done.40, f32[512,256]{1,0:T(8,128)S(1)} %copy-done.43, f32[512,256]{1,0:T(8,128)S(1)} %copy-done.48, ...), custom_call_target="tpu_custom_call" | custom-call | flops 3221225 | bytes 4194 | tf_op jit(solution)/shard_map/cycle_part/pallas_call | solution.py:199
  90.8 1.6 collective-permute-start.18
  92.9 1.6 collective-permute-start.13
  94.9 10.8 %collective-permute-done.18.refs_1_ = f32[512,256]{1,0:T(8,128)} collective-permute-done((f32[512,256]{1,0:T(8,128)S(1)}, f32[512,256]{1,0:T(8,128)}, u32[]{:S(2)}, u32[]{:S(2)}) %collective-permute-start.18) | collective-permute-done | bytes 524320 | tf_op jit(solution)/shard_map/ppermute | solution.py:403
  105.7 1.6 collective-permute-done.19.refs_2_
  107.3 1.5 collective-permute-start.20
  109.4 1.0 copy-done.11
  111.5 1.0 copy-done.38
  112.5 1.0 copy-done.41
  115.6 8.1 %ladder_part.4.refs_10_ = f32[16,128,256]{2,1,0:T(8,128)} custom-call(s32[8]{0:T(128)S(1)} %gather_fusion, s32[256]{0:T(256)S(1)} %reshape.57.index_ref, f32[512,256]{1,0:T(8,128)S(1)} %bitcast.13, f32[512,256]{1,0:T(8,128)S(1)} %copy-done.38, f32[512,256]{1,0:T(8,128)S(1)} %copy-done.41, f32[512,256]{1,0:T(8,128)S(1)} %copy-done.44, ...), custom_call_target="tpu_custom_call" | custom-call | flops 1610612 | bytes 4194 | tf_op jit(solution)/shard_map/ladder_part/pallas_call | solution.py:273
  124.8 1.5 collective-permute-start.15
  127.9 1.1 slice_add_fusion.3
  129.7 1.5 collective-permute-start.22
  131.2 2.9 %collective-permute-done.15.refs_7_ = f32[256,256]{1,0:T(8,128)S(1)} collective-permute-done((f32[256,256]{1,0:T(8,128)S(1)}, f32[256,256]{1,0:T(8,128)S(1)}, u32[]{:S(2)}, u32[]{:S(2)}) %collective-permute-start.15) | collective-permute-done | bytes 262176 | tf_op jit(solution)/shard_map/ppermute | solution.py:403
  134.6 8.1 %cycle_part.5 = (f32[256,1024]{1,0:T(8,128)S(1)}, f32[256,1024]{1,0:T(8,128)S(1)}) custom-call(s32[8]{0:T(128)S(1)} %gather_fusion, f32[512,256]{1,0:T(8,128)S(1)} %bitcast.24, f32[512,256]{1,0:T(8,128)} %collective-permute-done.9.refs_1_, f32[512,256]{1,0:T(8,128)} %collective-permute-done.10.refs_2_, f32[512,256]{1,0:T(8,128)} %collective-permute-done.11.refs_3_, ...), custom_call_target="tpu_custom_call" | custom-call | flops 3221225 | bytes 4194 | tf_op jit(solution)/shard_map/cycle_part/pallas_call | solution.py:199
  143.2 1.5 collective-permute-start.24
  144.8 1.6 collective-permute-start.28
  146.8 9.6 %ladder_part.5.refs_10_ = f32[16,128,256]{2,1,0:T(8,128)} custom-call(s32[8]{0:T(128)S(1)} %gather_fusion, s32[256]{0:T(256)S(1)} %reshape.57.index_ref, f32[512,256]{1,0:T(8,128)S(1)} %bitcast.25, f32[512,256]{1,0:T(8,128)} %collective-permute-done.9.refs_1_, f32[512,256]{1,0:T(8,128)} %collective-permute-done.10.refs_2_, ...), custom_call_target="tpu_custom_call", output_to_operand_aliasing={{}: (12, {})} | custom-call | flops 1610612 | bytes 4194 | tf_op jit(solution)/shard_map/ladder_part/pallas_call | solution.py:273
  156.4 1.3 collective-permute-done.23.refs_6_
  157.7 1.5 collective-permute-start.25
  159.9 9.1 %collective-permute-done.29.refs_2_ = f32[512,256]{1,0:T(8,128)S(1)} collective-permute-done((f32[512,256]{1,0:T(8,128)S(1)}, f32[512,256]{1,0:T(8,128)S(1)}, u32[]{:S(2)}, u32[]{:S(2)}) %collective-permute-start.29) | collective-permute-done | bytes 524320 | tf_op jit(solution)/shard_map/ppermute | solution.py:404
  168.9 1.5 collective-permute-start.30
  172.0 2.6 collective-permute-done.26.refs_8_
  174.6 7.7 %cycle_part.6 = (f32[256,1024]{1,0:T(8,128)S(1)}, f32[256,1024]{1,0:T(8,128)S(1)}) custom-call(s32[8]{0:T(128)S(1)} %gather_fusion, f32[512,256]{1,0:T(8,128)S(1)} %bitcast.20, f32[512,256]{1,0:T(8,128)} %collective-permute-done.18.refs_1_, f32[512,256]{1,0:T(8,128)} %collective-permute-done.19.refs_2_, f32[512,256]{1,0:T(8,128)} %collective-permute-done.20.refs_3_, ...), custom_call_target="tpu_custom_call" | custom-call | flops 3221225 | bytes 4194 | tf_op jit(solution)/shard_map/cycle_part/pallas_call | solution.py:199
  182.4 1.6 collective-permute-start.34
  184.0 1.3 collective-permute-done.31.refs_4_
  185.4 1.5 collective-permute-start.32
  187.4 9.4 %collective-permute-done.34.refs_5_ = f32[128,1024]{1,0:T(8,128)S(1)} collective-permute-done((f32[128,1024]{1,0:T(8,128)S(1)}, f32[128,1024]{1,0:T(8,128)S(1)}, u32[]{:S(2)}, u32[]{:S(2)}) %collective-permute-start.34) | collective-permute-done | bytes 524320 | tf_op jit(solution)/shard_map/ppermute | solution.py:432
  196.8 2.1 collective-permute-done.32.refs_5_
  198.8 1.2 collective-permute-done.33.refs_6_
  200.8 1.6 collective-permute-start.36
  203.4 9.3 %ladder_part.6.refs_6_ = f32[16,128,256]{2,1,0:T(8,128)} custom-call(s32[8]{0:T(128)S(1)} %gather_fusion, s32[256]{0:T(256)S(1)} %reshape.57.index_ref, f32[512,256]{1,0:T(8,128)S(1)} %bitcast.21, f32[512,256]{1,0:T(8,128)} %collective-permute-done.18.refs_1_, f32[512,256]{1,0:T(8,128)} %collective-permute-done.19.refs_2_, ...), custom_call_target="tpu_custom_call", output_to_operand_aliasing={{}: (12, {})} | custom-call | flops 1610612 | bytes 4194 | tf_op jit(solution)/shard_map/ladder_part/pallas_call | solution.py:273
  212.8 7.8 %cycle_part.7 = (f32[256,1024]{1,0:T(8,128)S(1)}, f32[256,1024]{1,0:T(8,128)}) custom-call(s32[8]{0:T(128)S(1)} %gather_fusion, f32[512,256]{1,0:T(8,128)S(1)} %bitcast.16, f32[512,256]{1,0:T(8,128)S(1)} %collective-permute-done.28.refs_1_, f32[512,256]{1,0:T(8,128)S(1)} %collective-permute-done.29.refs_2_, f32[512,256]{1,0:T(8,128)S(1)} %collective-permute-done.30.refs_3_, ...), custom_call_target="tpu_custom_call" | custom-call | flops 3221225 | bytes 4194 | tf_op jit(solution)/shard_map/cycle_part/pallas_call | solution.py:199
  222.4 1.5 collective-permute-start.38
  224.4 1.2 copy-done.21
  225.7 5.1 %join.4.refs_6_ = f32[16,128,256]{2,1,0:T(8,128)} custom-call(f32[16,256]{1,0:T(8,128)S(1)} %broadcast_in_dim.6.refs_0_.refs_11_, f32[128,256]{1,0:T(8,128)S(1)} %broadcast_in_dim.7.refs_1_.refs_12_, f32[1,256]{1,0:T(1,128)S(1)} %add.65.refs_2_.refs_13_, f32[256,1024]{1,0:T(8,128)S(1)} %copy-done.21, ...), custom_call_target="tpu_custom_call", output_to_operand_aliasing={{}: (6, {})} | custom-call | flops 1048 | bytes 2621 | tf_op jit(solution)/shard_map/join/pallas_call | solution.py:326
  230.8 4.8 %join.5.refs_6_ = f32[16,128,256]{2,1,0:T(8,128)} custom-call(f32[16,256]{1,0:T(8,128)S(1)} %broadcast_in_dim.6.refs_0_.refs_11_, f32[128,256]{1,0:T(8,128)S(1)} %broadcast_in_dim.7.refs_1_.refs_12_, f32[1,256]{1,0:T(1,128)S(1)} %add.65.refs_2_.refs_13_, f32[256,1024]{1,0:T(8,128)S(1)} %copy-done.23, ...), custom_call_target="tpu_custom_call", output_to_operand_aliasing={{}: (6, {})} | custom-call | flops 1048 | bytes 2621 | tf_op jit(solution)/shard_map/join/pallas_call | solution.py:326
  235.7 1.3 collective-permute-done.38.refs_5_
  238.0 1.6 collective-permute-start.39
  239.5 1.0 copy-done.59
  240.6 4.7 %join.6.refs_10_ = f32[16,128,256]{2,1,0:T(8,128)} custom-call(f32[16,256]{1,0:T(8,128)S(1)} %broadcast_in_dim.6.refs_0_.refs_11_, f32[128,256]{1,0:T(8,128)S(1)} %broadcast_in_dim.7.refs_1_.refs_12_, f32[1,256]{1,0:T(1,128)S(1)} %add.65.refs_2_.refs_13_, f32[256,1024]{1,0:T(8,128)S(1)} %copy-done.27, ...), custom_call_target="tpu_custom_call", output_to_operand_aliasing={{}: (6, {})} | custom-call | flops 1048 | bytes 2621 | tf_op jit(solution)/shard_map/join/pallas_call | solution.py:326
  245.3 8.7 %ladder_part.7.refs_6_ = f32[16,128,256]{2,1,0:T(8,128)} custom-call(s32[8]{0:T(128)S(1)} %gather_fusion, s32[256]{0:T(256)S(1)} %reshape.57.index_ref, f32[512,256]{1,0:T(8,128)S(1)} %bitcast.17, f32[512,256]{1,0:T(8,128)S(1)} %copy-done.33, f32[512,256]{1,0:T(8,128)S(1)} %copy-done.35, f32[512,256]{1,0:T(8,128)S(1)} %copy-done.46, ...), custom_call_target="tpu_custom_call", output_to_operand_aliasing={{}: (12, {})} | custom-call | flops 1610612 | bytes 4194 | tf_op jit(solution)/shard_map/ladder_part/pallas_call | solution.py:273
  254.0 4.8 %join.7 = f32[16,128,256]{2,1,0:T(8,128)} custom-call(f32[16,256]{1,0:T(8,128)S(1)} %broadcast_in_dim.6.refs_0_.refs_11_, f32[128,256]{1,0:T(8,128)S(1)} %broadcast_in_dim.7.refs_1_.refs_12_, f32[1,256]{1,0:T(1,128)S(1)} %add.65.refs_2_.refs_13_, f32[256,1024]{1,0:T(8,128)S(1)} %copy-done.31, ...), custom_call_target="tpu_custom_call", output_to_operand_aliasing={{}: (6, {})} | custom-call | flops 1048 | bytes 2621 | tf_op jit(solution)/shard_map/join/pallas_call | solution.py:326
  (201 shorter events, 25.1 us)
Async XLA Ops:
  6.5 66.3 %all-gather.5.cloned.1.call-start = ((), (), s32[]{:S(2)}) async-start(), calls=%async_computation | async-start | bytes 5242880 | tf_op jit(solution)/shard_map/all_gather | solution.py:481
  7.6 15.7 %copy-start.2 = (f32[16,32,256]{2,1,0:T(8,128)}, f32[16,32,256]{2,1,0:T(8,128)S(1)}, u32[]{:S(2)}) copy-start(f32[16,32,256]{2,1,0:T(8,128)S(1)} %slice.82) | copy-start | bytes 1572868
  10.2 14.9 %collective-permute-start = (f32[512,256]{1,0:T(8,128)S(1)}, f32[512,256]{1,0:T(8,128)S(1)}, u32[]{:S(2)}, u32[]{:S(2)}) collective-permute-start(f32[512,256]{1,0:T(8,128)S(1)} %bitcast.10), channel_id=1, source_target_pairs={{0,8},{8,16},{16,24},{24,28},{28,20},{20,12},{12,4},{4,0},{1,9},{9... | collective-permute-start | bytes 1572872 | tf_op jit(solution)/shard_map/ppermute | solution.py:403
  13.3 13.4 %collective-permute-start.1 = (f32[512,256]{1,0:T(8,128)S(1)}, f32[512,256]{1,0:T(8,128)S(1)}, u32[]{:S(2)}, u32[]{:S(2)}) collective-permute-start(f32[512,256]{1,0:T(8,128)S(1)} %bitcast.11), channel_id=1, source_target_pairs={{8,0},{16,8},{24,16},{28,24},{20,28},{12,20},{4,12},{0,4},{9,1},{1... | collective-permute-start | bytes 1572872 | tf_op jit(solution)/shard_map/ppermute | solution.py:404
  23.3 19.3 %copy-start.61 = (f32[2048,256]{1,0:T(8,128)S(1)}, f32[2048,256]{1,0:T(8,128)}, u32[]{:S(2)}) copy-start(f32[2048,256]{1,0:T(8,128)} %param.10) | copy-start | bytes 6291460
  26.6 12.6 %collective-permute-start.2 = (f32[512,256]{1,0:T(8,128)S(1)}, f32[512,256]{1,0:T(8,128)S(1)}, u32[]{:S(2)}, u32[]{:S(2)}) collective-permute-start(f32[512,256]{1,0:T(8,128)S(1)} %collective-permute-done.refs_1_), channel_id=1, source_target_pairs={{0,8},{8,16},{16,24},{24,28},{28,20},{20,12},{12,4},{4,0},{1,9},{9... | collective-permute-start | bytes 1572872 | tf_op jit(solution)/shard_map/ppermute | solution.py:403
  28.2 12.3 %collective-permute-start.3 = (f32[512,256]{1,0:T(8,128)S(1)}, f32[512,256]{1,0:T(8,128)S(1)}, u32[]{:S(2)}, u32[]{:S(2)}) collective-permute-start(f32[512,256]{1,0:T(8,128)S(1)} %collective-permute-done.1.refs_2_), channel_id=1, source_target_pairs={{8,0},{16,8},{24,16},{28,24},{20,28},{12,20},{4,12},{0,4},{9,1},{1... | collective-permute-start | bytes 1572872 | tf_op jit(solution)/shard_map/ppermute | solution.py:404
  32.8 12.7 %copy-start.63 = (s32[32,4]{0,1:T(4,128)S(1)}, s32[32,4]{0,1:T(4,128)}, u32[]{:S(2)}) copy-start(s32[32,4]{0,1:T(4,128)} %param.14) | copy-start | bytes 1540
  32.9 18.0 %copy-start.67 = (s32[8]{0:T(128)S(1)}, s32[8]{0:T(128)}, u32[]{:S(2)}) copy-start(s32[8]{0:T(128)} %constant.40.clone) | copy-start | bytes 100
  39.2 22.3 %copy-start.42 = (f32[512,256]{1,0:T(8,128)}, f32[512,256]{1,0:T(8,128)S(1)}, u32[]{:S(2)}) copy-start(f32[512,256]{1,0:T(8,128)S(1)} %collective-permute-done.2.refs_3_) | copy-start | bytes 1572868
  40.5 21.0 %copy-start.47 = (f32[512,256]{1,0:T(8,128)}, f32[512,256]{1,0:T(8,128)S(1)}, u32[]{:S(2)}) copy-start(f32[512,256]{1,0:T(8,128)S(1)} %collective-permute-done.3.refs_4_) | copy-start | bytes 1572868
  40.5 25.3 %collective-permute-start.4 = (f32[512,256]{1,0:T(8,128)S(1)}, f32[512,256]{1,0:T(8,128)S(1)}, u32[]{:S(2)}, u32[]{:S(2)}) collective-permute-start(f32[512,256]{1,0:T(8,128)S(1)} %collective-permute-done.2.refs_3_), channel_id=1, source_target_pairs={{0,8},{8,16},{16,24},{24,28},{28,20},{20,12},{12,4},{4,0},{1,9},{9... | collective-permute-start | bytes 1572872 | tf_op jit(solution)/shard_map/ppermute | solution.py:403
  42.1 23.7 %collective-permute-start.5 = (f32[512,256]{1,0:T(8,128)S(1)}, f32[512,256]{1,0:T(8,128)S(1)}, u32[]{:S(2)}, u32[]{:S(2)}) collective-permute-start(f32[512,256]{1,0:T(8,128)S(1)} %collective-permute-done.3.refs_4_), channel_id=1, source_target_pairs={{8,0},{16,8},{24,16},{28,24},{20,28},{12,20},{4,12},{0,4},{9,1},{1... | collective-permute-start | bytes 1572872 | tf_op jit(solution)/shard_map/ppermute | solution.py:404
  43.5 18.1 %copy-start.6 = (f32[16,32,256]{2,1,0:T(8,128)}, f32[16,32,256]{2,1,0:T(8,128)S(1)}, u32[]{:S(2)}) copy-start(f32[16,32,256]{2,1,0:T(8,128)S(1)} %get-tuple-element.125) | copy-start | bytes 1572868
  43.5 27.3 %collective-permute-start.9 = (f32[512,256]{1,0:T(8,128)S(1)}, f32[512,256]{1,0:T(8,128)}, u32[]{:S(2)}, u32[]{:S(2)}) collective-permute-start(f32[512,256]{1,0:T(8,128)S(1)} %bitcast.22), channel_id=1, source_target_pairs={{0,8},{8,16},{16,24},{24,28},{28,20},{20,12},{12,4},{4,0},{1,9},{9... | collective-permute-start | bytes 1572872 | tf_op jit(solution)/shard_map/ppermute | solution.py:403
  45.1 25.7 %collective-permute-start.10 = (f32[512,256]{1,0:T(8,128)S(1)}, f32[512,256]{1,0:T(8,128)}, u32[]{:S(2)}, u32[]{:S(2)}) collective-permute-start(f32[512,256]{1,0:T(8,128)S(1)} %bitcast.23), channel_id=1, source_target_pairs={{8,0},{16,8},{24,16},{28,24},{20,28},{12,20},{4,12},{0,4},{9,1},{1... | collective-permute-start | bytes 1572872 | tf_op jit(solution)/shard_map/ppermute | solution.py:404
  66.6 14.9 %collective-permute-start.6 = (f32[256,256]{1,0:T(8,128)}, f32[256,256]{1,0:T(8,128)S(1)}, u32[]{:S(2)}, u32[]{:S(2)}) collective-permute-start(f32[256,256]{1,0:T(8,128)} %slice.64), channel_id=1, source_target_pairs={{0,8},{8,16},{16,24},{24,28},{28,20},{20,12},{12,4},{4,0},{1,9},{9... | collective-permute-start | bytes 786440 | tf_op jit(solution)/shard_map/ppermute | solution.py:403
  68.9 12.6 %collective-permute-start.7 = (f32[256,256]{1,0:T(8,128)}, f32[256,256]{1,0:T(8,128)}, u32[]{:S(2)}, u32[]{:S(2)}) collective-permute-start(f32[256,256]{1,0:T(8,128)} %slice.65), channel_id=1, source_target_pairs={{8,0},{16,8},{24,16},{28,24},{20,28},{12,20},{4,12},{0,4},{9,1},{1... | collective-permute-start | bytes 786440 | tf_op jit(solution)/shard_map/ppermute | solution.py:404
  70.7 22.1 %collective-permute-start.11 = (f32[512,256]{1,0:T(8,128)}, f32[512,256]{1,0:T(8,128)}, u32[]{:S(2)}, u32[]{:S(2)}) collective-permute-start(f32[512,256]{1,0:T(8,128)} %collective-permute-done.9.refs_1_), channel_id=1, source_target_pairs={{0,8},{8,16},{16,24},{24,28},{28,20},{20,12},{12,4},{4,0},{1,9},{9... | collective-permute-start | bytes 1572872 | tf_op jit(solution)/shard_map/ppermute | solution.py:403
  72.4 20.5 %collective-permute-start.12 = (f32[512,256]{1,0:T(8,128)}, f32[512,256]{1,0:T(8,128)}, u32[]{:S(2)}, u32[]{:S(2)}) collective-permute-start(f32[512,256]{1,0:T(8,128)} %collective-permute-done.10.refs_2_), channel_id=1, source_target_pairs={{8,0},{16,8},{24,16},{28,24},{20,28},{12,20},{4,12},{0,4},{9,1},{1... | collective-permute-start | bytes 1572872 | tf_op jit(solution)/shard_map/ppermute | solution.py:404
  81.6 27.7 %copy-start.62 = (s32[16,16]{1,0:T(8,128)S(1)}, s32[16,16]{1,0:T(8,128)}, u32[]{:S(2)}) copy-start(s32[16,16]{1,0:T(8,128)} %param.12) | copy-start | bytes 3076
  90.8 37.1 %collective-permute-start.8 = (f32[256,1024]{1,0:T(8,128)}, f32[256,1024]{1,0:T(8,128)}, u32[]{:S(2)}, u32[]{:S(2)}) collective-permute-start(f32[256,1024]{1,0:T(8,128)} %get-tuple-element.83), channel_id=1, source_target_pairs={{0,1},{1,0},{2,3},{3,2},{4,5},{5,4},{6,7},{7,6},{8,9},{9,8},{10,11... | collective-permute-start | bytes 3145736 | tf_op jit(solution)/shard_map/ppermute | solution.py:424
  90.8 14.8 %collective-permute-start.18 = (f32[512,256]{1,0:T(8,128)S(1)}, f32[512,256]{1,0:T(8,128)}, u32[]{:S(2)}, u32[]{:S(2)}) collective-permute-start(f32[512,256]{1,0:T(8,128)S(1)} %bitcast.18), channel_id=1, source_target_pairs={{0,8},{8,16},{16,24},{24,28},{28,20},{20,12},{12,4},{4,0},{1,9},{9... | collective-permute-start | bytes 1572872 | tf_op jit(solution)/shard_map/ppermute | solution.py:403
  92.4 14.9 %collective-permute-start.19 = (f32[512,256]{1,0:T(8,128)S(1)}, f32[512,256]{1,0:T(8,128)}, u32[]{:S(2)}, u32[]{:S(2)}) collective-permute-start(f32[512,256]{1,0:T(8,128)S(1)} %bitcast.19), channel_id=1, source_target_pairs={{8,0},{16,8},{24,16},{28,24},{20,28},{12,20},{4,12},{0,4},{9,1},{1... | collective-permute-start | bytes 1572872 | tf_op jit(solution)/shard_map/ppermute | solution.py:404
  92.9 30.9 %collective-permute-start.13 = (f32[512,256]{1,0:T(8,128)}, f32[512,256]{1,0:T(8,128)}, u32[]{:S(2)}, u32[]{:S(2)}) collective-permute-start(f32[512,256]{1,0:T(8,128)} %collective-permute-done.11.refs_3_), channel_id=1, source_target_pairs={{0,8},{8,16},{16,24},{24,28},{28,20},{20,12},{12,4},{4,0},{1,9},{9... | collective-permute-start | bytes 1572872 | tf_op jit(solution)/shard_map/ppermute | solution.py:403
  94.4 29.3 %collective-permute-start.14 = (f32[512,256]{1,0:T(8,128)}, f32[512,256]{1,0:T(8,128)}, u32[]{:S(2)}, u32[]{:S(2)}) collective-permute-start(f32[512,256]{1,0:T(8,128)} %collective-permute-done.12.refs_4_), channel_id=1, source_target_pairs={{8,0},{16,8},{24,16},{28,24},{20,28},{12,20},{4,12},{0,4},{9,1},{1... | collective-permute-start | bytes 1572872 | tf_op jit(solution)/shard_map/ppermute | solution.py:404
  107.3 21.8 %collective-permute-start.20 = (f32[512,256]{1,0:T(8,128)}, f32[512,256]{1,0:T(8,128)}, u32[]{:S(2)}, u32[]{:S(2)}) collective-permute-start(f32[512,256]{1,0:T(8,128)} %collective-permute-done.18.refs_1_), channel_id=1, source_target_pairs={{0,8},{8,16},{16,24},{24,28},{28,20},{20,12},{12,4},{4,0},{1,9},{9... | collective-permute-start | bytes 1572872 | tf_op jit(solution)/shard_map/ppermute | solution.py:403
  108.8 21.0 %collective-permute-start.21 = (f32[512,256]{1,0:T(8,128)}, f32[512,256]{1,0:T(8,128)}, u32[]{:S(2)}, u32[]{:S(2)}) collective-permute-start(f32[512,256]{1,0:T(8,128)} %collective-permute-done.19.refs_2_), channel_id=1, source_target_pairs={{8,0},{16,8},{24,16},{28,24},{20,28},{12,20},{4,12},{0,4},{9,1},{1... | collective-permute-start | bytes 1572872 | tf_op jit(solution)/shard_map/ppermute | solution.py:404
  115.6 12.3 %copy-start.20 = (f32[256,1024]{1,0:T(8,128)S(1)}, f32[256,1024]{1,0:T(8,128)}, u32[]{:S(2)}) copy-start(f32[256,1024]{1,0:T(8,128)} %copy-done.19) | copy-start | bytes 3145732
  123.7 10.8 %copy-start.7 = (f32[16,32,256]{2,1,0:T(8,128)S(1)}, f32[16,32,256]{2,1,0:T(8,128)}, u32[]{:S(2)}) copy-start(f32[16,32,256]{2,1,0:T(8,128)} %copy-done.6) | copy-start | bytes 1572868
  124.8 9.3 %collective-permute-start.15 = (f32[256,256]{1,0:T(8,128)S(1)}, f32[256,256]{1,0:T(8,128)S(1)}, u32[]{:S(2)}, u32[]{:S(2)}) collective-permute-start(f32[256,256]{1,0:T(8,128)S(1)} %slice.68), channel_id=1, source_target_pairs={{0,8},{8,16},{16,24},{24,28},{28,20},{20,12},{12,4},{4,0},{1,9},{9... | collective-permute-start | bytes 786440 | tf_op jit(solution)/shard_map/ppermute | solution.py:403
  127.3 7.2 %collective-permute-start.16 = (f32[256,256]{1,0:T(8,128)S(1)}, f32[256,256]{1,0:T(8,128)S(1)}, u32[]{:S(2)}, u32[]{:S(2)}) collective-permute-start(f32[256,256]{1,0:T(8,128)S(1)} %slice.69), channel_id=1, source_target_pairs={{8,0},{16,8},{24,16},{28,24},{20,28},{12,20},{4,12},{0,4},{9,1},{1... | collective-permute-start | bytes 786440 | tf_op jit(solution)/shard_map/ppermute | solution.py:404
  129.7 16.6 %collective-permute-start.22 = (f32[512,256]{1,0:T(8,128)}, f32[512,256]{1,0:T(8,128)S(1)}, u32[]{:S(2)}, u32[]{:S(2)}) collective-permute-start(f32[512,256]{1,0:T(8,128)} %collective-permute-done.20.refs_3_), channel_id=1, source_target_pairs={{0,8},{8,16},{16,24},{24,28},{28,20},{20,12},{12,4},{4,0},{1,9},{9... | collective-permute-start | bytes 1572872 | tf_op jit(solution)/shard_map/ppermute | solution.py:403
  142.6 28.3 %copy-start.22 = (f32[256,1024]{1,0:T(8,128)}, f32[256,1024]{1,0:T(8,128)S(1)}, u32[]{:S(2)}) copy-start(f32[256,1024]{1,0:T(8,128)S(1)} %get-tuple-element.95.refs_3_) | copy-start | bytes 3145732
  142.6 28.3 %collective-permute-start.17 = (f32[256,1024]{1,0:T(8,128)S(1)}, f32[256,1024]{1,0:T(8,128)S(1)}, u32[]{:S(2)}, u32[]{:S(2)}) collective-permute-start(f32[256,1024]{1,0:T(8,128)S(1)} %get-tuple-element.96), channel_id=1, source_target_pairs={{0,1},{1,0},{2,3},{3,2},{4,5},{5,4},{6,7},{7,6},{8,9},{9,8},{10,11... | collective-permute-start | bytes 3145736 | tf_op jit(solution)/shard_map/ppermute | solution.py:424
  142.7 15.0 %collective-permute-start.23 = (f32[512,256]{1,0:T(8,128)}, f32[512,256]{1,0:T(8,128)S(1)}, u32[]{:S(2)}, u32[]{:S(2)}) collective-permute-start(f32[512,256]{1,0:T(8,128)} %collective-permute-done.21.refs_4_), channel_id=1, source_target_pairs={{8,0},{16,8},{24,16},{28,24},{20,28},{12,20},{4,12},{0,4},{9,1},{1... | collective-permute-start | bytes 1572872 | tf_op jit(solution)/shard_map/ppermute | solution.py:404
  143.2 14.5 %collective-permute-start.24 = (f32[128,1024]{1,0:T(8,128)S(1)}, f32[128,1024]{1,0:T(8,128)S(1)}, u32[]{:S(2)}, u32[]{:S(2)}) collective-permute-start(f32[128,1024]{1,0:T(8,128)S(1)} %slice_add_fusion.3), channel_id=1, source_target_pairs={{0,2},{1,3},{2,0},{3,1},{4,6},{5,7},{6,4},{7,5},{8,10},{9,11},{10,... | collective-permute-start | bytes 1572872 | tf_op jit(solution)/shard_map/ppermute | solution.py:432
  144.8 15.1 %collective-permute-start.28 = (f32[512,256]{1,0:T(8,128)S(1)}, f32[512,256]{1,0:T(8,128)S(1)}, u32[]{:S(2)}, u32[]{:S(2)}) collective-permute-start(f32[512,256]{1,0:T(8,128)S(1)} %bitcast.14), channel_id=1, source_target_pairs={{0,8},{8,16},{16,24},{24,28},{28,20},{20,12},{12,4},{4,0},{1,9},{9... | collective-permute-start | bytes 1572872 | tf_op jit(solution)/shard_map/ppermute | solution.py:403
  146.3 22.6 %collective-permute-start.29 = (f32[512,256]{1,0:T(8,128)S(1)}, f32[512,256]{1,0:T(8,128)S(1)}, u32[]{:S(2)}, u32[]{:S(2)}) collective-permute-start(f32[512,256]{1,0:T(8,128)S(1)} %bitcast.15), channel_id=1, source_target_pairs={{8,0},{16,8},{24,16},{28,24},{20,28},{12,20},{4,12},{0,4},{9,1},{1... | collective-permute-start | bytes 1572872 | tf_op jit(solution)/shard_map/ppermute | solution.py:404
  156.4 18.1 %copy-start.5 = (f32[16,32,256]{2,1,0:T(8,128)S(1)}, f32[16,32,256]{2,1,0:T(8,128)}, u32[]{:S(2)}) copy-start(f32[16,32,256]{2,1,0:T(8,128)} %get-tuple-element.126) | copy-start | bytes 1572868
  157.7 14.3 %copy-start.54 = (f32[128,1024]{1,0:T(8,128)}, f32[128,1024]{1,0:T(8,128)S(1)}, u32[]{:S(2)}) copy-start(f32[128,1024]{1,0:T(8,128)S(1)} %collective-permute-done.24.refs_5_) | copy-start | bytes 1572868
  157.7 14.2 %collective-permute-start.25 = (f32[256,256]{1,0:T(8,128)S(1)}, f32[256,256]{1,0:T(8,128)S(1)}, u32[]{:S(2)}, u32[]{:S(2)}) collective-permute-start(f32[256,256]{1,0:T(8,128)S(1)} %slice.72), channel_id=1, source_target_pairs={{0,8},{8,16},{16,24},{24,28},{28,20},{20,12},{12,4},{4,0},{1,9},{9... | collective-permute-start | bytes 786440 | tf_op jit(solution)/shard_map/ppermute | solution.py:403
  159.3 15.3 %collective-permute-start.26 = (f32[256,256]{1,0:T(8,128)S(1)}, f32[256,256]{1,0:T(8,128)S(1)}, u32[]{:S(2)}, u32[]{:S(2)}) collective-permute-start(f32[256,256]{1,0:T(8,128)S(1)} %slice.73), channel_id=1, source_target_pairs={{8,0},{16,8},{24,16},{28,24},{20,28},{12,20},{4,12},{0,4},{9,1},{1... | collective-permute-start | bytes 786440 | tf_op jit(solution)/shard_map/ppermute | solution.py:404
  159.9 52.9 %copy-start.32 = (f32[512,256]{1,0:T(8,128)}, f32[512,256]{1,0:T(8,128)S(1)}, u32[]{:S(2)}) copy-start(f32[512,256]{1,0:T(8,128)S(1)} %collective-permute-done.28.refs_1_) | copy-start | bytes 1572868
  168.9 15.1 %collective-permute-start.30 = (f32[512,256]{1,0:T(8,128)S(1)}, f32[512,256]{1,0:T(8,128)S(1)}, u32[]{:S(2)}, u32[]{:S(2)}) collective-permute-start(f32[512,256]{1,0:T(8,128)S(1)} %collective-permute-done.28.refs_1_), channel_id=1, source_target_pairs={{0,8},{8,16},{16,24},{24,28},{28,20},{20,12},{12,4},{4,0},{1,9},{9... | collective-permute-start | bytes 1572872 | tf_op jit(solution)/shard_map/ppermute | solution.py:403
  170.4 14.9 %collective-permute-start.31 = (f32[512,256]{1,0:T(8,128)S(1)}, f32[512,256]{1,0:T(8,128)S(1)}, u32[]{:S(2)}, u32[]{:S(2)}) collective-permute-start(f32[512,256]{1,0:T(8,128)S(1)} %collective-permute-done.29.refs_2_), channel_id=1, source_target_pairs={{8,0},{16,8},{24,16},{28,24},{20,28},{12,20},{4,12},{0,4},{9,1},{1... | collective-permute-start | bytes 1572872 | tf_op jit(solution)/shard_map/ppermute | solution.py:404
  182.3 30.4 %copy-start.26 = (f32[256,1024]{1,0:T(8,128)}, f32[256,1024]{1,0:T(8,128)S(1)}, u32[]{:S(2)}) copy-start(f32[256,1024]{1,0:T(8,128)S(1)} %get-tuple-element.107.refs_3_) | copy-start | bytes 3145732
  182.3 20.1 %collective-permute-start.27 = (f32[256,1024]{1,0:T(8,128)S(1)}, f32[256,1024]{1,0:T(8,128)S(1)}, u32[]{:S(2)}, u32[]{:S(2)}) collective-permute-start(f32[256,1024]{1,0:T(8,128)S(1)} %get-tuple-element.108), channel_id=1, source_target_pairs={{0,1},{1,0},{2,3},{3,2},{4,5},{5,4},{6,7},{7,6},{8,9},{9,8},{10,11... | collective-permute-start | bytes 3145736 | tf_op jit(solution)/shard_map/ppermute | solution.py:424
  182.4 14.3 %collective-permute-start.34 = (f32[128,1024]{1,0:T(8,128)S(1)}, f32[128,1024]{1,0:T(8,128)S(1)}, u32[]{:S(2)}, u32[]{:S(2)}) collective-permute-start(f32[128,1024]{1,0:T(8,128)S(1)} %slice_add_fusion.2), channel_id=1, source_target_pairs={{0,2},{1,3},{2,0},{3,1},{4,6},{5,7},{6,4},{7,5},{8,10},{9,11},{10,... | collective-permute-start | bytes 1572872 | tf_op jit(solution)/shard_map/ppermute | solution.py:432
  184.0 28.8 %copy-start.45 = (f32[512,256]{1,0:T(8,128)}, f32[512,256]{1,0:T(8,128)S(1)}, u32[]{:S(2)}) copy-start(f32[512,256]{1,0:T(8,128)S(1)} %collective-permute-done.30.refs_3_) | copy-start | bytes 1572868
  185.4 27.5 %copy-start.50 = (f32[512,256]{1,0:T(8,128)}, f32[512,256]{1,0:T(8,128)S(1)}, u32[]{:S(2)}) copy-start(f32[512,256]{1,0:T(8,128)S(1)} %collective-permute-done.31.refs_4_) | copy-start | bytes 1572868
  185.4 13.5 %collective-permute-start.32 = (f32[512,256]{1,0:T(8,128)S(1)}, f32[512,256]{1,0:T(8,128)S(1)}, u32[]{:S(2)}, u32[]{:S(2)}) collective-permute-start(f32[512,256]{1,0:T(8,128)S(1)} %collective-permute-done.30.refs_3_), channel_id=1, source_target_pairs={{0,8},{8,16},{16,24},{24,28},{28,20},{20,12},{12,4},{4,0},{1,9},{9... | collective-permute-start | bytes 1572872 | tf_op jit(solution)/shard_map/ppermute | solution.py:403
  186.8 13.2 %collective-permute-start.33 = (f32[512,256]{1,0:T(8,128)S(1)}, f32[512,256]{1,0:T(8,128)S(1)}, u32[]{:S(2)}, u32[]{:S(2)}) collective-permute-start(f32[512,256]{1,0:T(8,128)S(1)} %collective-permute-done.31.refs_4_), channel_id=1, source_target_pairs={{8,0},{16,8},{24,16},{28,24},{20,28},{12,20},{4,12},{0,4},{9,1},{1... | collective-permute-start | bytes 1572872 | tf_op jit(solution)/shard_map/ppermute | solution.py:404
  196.8 16.0 %copy-start.56 = (f32[128,1024]{1,0:T(8,128)}, f32[128,1024]{1,0:T(8,128)S(1)}, u32[]{:S(2)}) copy-start(f32[128,1024]{1,0:T(8,128)S(1)} %collective-permute-done.34.refs_5_) | copy-start | bytes 1572868
  198.8 14.0 %copy-start.15 = (f32[512,256]{1,0:T(8,128)}, f32[512,256]{1,0:T(8,128)S(1)}, u32[]{:S(2)}) copy-start(f32[512,256]{1,0:T(8,128)S(1)} %collective-permute-done.32.refs_5_) | copy-start | bytes 1572868
  200.1 12.8 %copy-start.17 = (f32[512,256]{1,0:T(8,128)}, f32[512,256]{1,0:T(8,128)S(1)}, u32[]{:S(2)}) copy-start(f32[512,256]{1,0:T(8,128)S(1)} %collective-permute-done.33.refs_6_) | copy-start | bytes 1572868
  200.1 12.7 %collective-permute-start.35 = (f32[256,256]{1,0:T(8,128)S(1)}, f32[256,256]{1,0:T(8,128)S(1)}, u32[]{:S(2)}, u32[]{:S(2)}) collective-permute-start(f32[256,256]{1,0:T(8,128)S(1)} %slice.76), channel_id=1, source_target_pairs={{0,8},{8,16},{16,24},{24,28},{28,20},{20,12},{12,4},{4,0},{1,9},{9... | collective-permute-start | bytes 786440 | tf_op jit(solution)/shard_map/ppermute | solution.py:403
  200.8 12.0 %collective-permute-start.36 = (f32[256,256]{1,0:T(8,128)S(1)}, f32[256,256]{1,0:T(8,128)S(1)}, u32[]{:S(2)}, u32[]{:S(2)}) collective-permute-start(f32[256,256]{1,0:T(8,128)S(1)} %slice.77), channel_id=1, source_target_pairs={{8,0},{16,8},{24,16},{28,24},{20,28},{12,20},{4,12},{0,4},{9,1},{1... | collective-permute-start | bytes 786440 | tf_op jit(solution)/shard_map/ppermute | solution.py:404
  212.7 11.2 %copy-start.64 = (f32[128]{0:T(128)S(1)}, f32[128]{0:T(128)}, u32[]{:S(2)}) copy-start(f32[128]{0:T(128)} %param.15) | copy-start | bytes 1540
  212.7 11.3 %copy-start.65 = (f32[32]{0:T(128)S(1)}, f32[32]{0:T(128)}, u32[]{:S(2)}) copy-start(f32[32]{0:T(128)} %param.16) | copy-start | bytes 388
  212.8 11.7 %copy-start.55 = (f32[128,1024]{1,0:T(8,128)S(1)}, f32[128,1024]{1,0:T(8,128)}, u32[]{:S(2)}) copy-start(f32[128,1024]{1,0:T(8,128)} %copy-done.54) | copy-start | bytes 1572868
  222.4 15.4 %collective-permute-start.37 = (f32[256,1024]{1,0:T(8,128)}, f32[256,1024]{1,0:T(8,128)S(1)}, u32[]{:S(2)}, u32[]{:S(2)}) collective-permute-start(f32[256,1024]{1,0:T(8,128)} %get-tuple-element.120), channel_id=1, source_target_pairs={{0,1},{1,0},{2,3},{3,2},{4,5},{5,4},{6,7},{7,6},{8,9},{9,8},{10,11... | collective-permute-start | bytes 3145736 | tf_op jit(solution)/shard_map/ppermute | solution.py:424
  222.4 14.5 %collective-permute-start.38 = (f32[128,1024]{1,0:T(8,128)}, f32[128,1024]{1,0:T(8,128)S(1)}, u32[]{:S(2)}, u32[]{:S(2)}) collective-permute-start(f32[128,1024]{1,0:T(8,128)} %slice_add_fusion.1), channel_id=1, source_target_pairs={{0,2},{1,3},{2,0},{3,1},{4,6},{5,7},{6,4},{7,5},{8,10},{9,11},{10,... | collective-permute-start | bytes 1572872 | tf_op jit(solution)/shard_map/ppermute | solution.py:432
  238.0 16.0 %collective-permute-start.39 = (f32[128,1024]{1,0:T(8,128)S(1)}, f32[128,1024]{1,0:T(8,128)S(1)}, u32[]{:S(2)}, u32[]{:S(2)}) collective-permute-start(f32[128,1024]{1,0:T(8,128)S(1)} %slice_add_fusion), channel_id=1, source_target_pairs={{0,2},{1,3},{2,0},{3,1},{4,6},{5,7},{6,4},{7,5},{8,10},{9,11},{10,... | collective-permute-start | bytes 1572872 | tf_op jit(solution)/shard_map/ppermute | solution.py:432
  (45 other events, 230.7 us)
Sparse Core Ops, SparseCore 0:
  10.3 37.1 all-gather.4
